TPU v7x, 512 devices: a whole 4x4x16 slice. The times are simulated.
512 devices in a mesh: head: 16 (over x_hi, y, core), ctx: 32 (over x_lo, z).
Axes of the slice: x: 4 (x_hi: 2, x_lo: 2; x = x_hi * 2 + x_lo), y: 4, z: 16, core: 2. Of those that a mesh axis runs over, the one named last changes fastest.
Arguments:
- queries: bfloat16 [64, 8192, 128], P('head', 'ctx'), may hold values from -8 to 8
- key_heads: bfloat16 [4, 8192, 128], P(None, 'ctx'), may hold values from -8 to 8
- value_heads: bfloat16 [4, 8192, 128], P(None, 'ctx'), may hold values from -6 to 6
- doc_lengths: int32 [16], replicated, may hold values from 1 to 4096, 8192 in all
- span_order: int32 [64], replicated, may hold values from 0 to 63, each once
Outputs:
- attended: bfloat16 [64, 8192, 128], P('head', 'ctx')
All inputs are finite; a program needn't handle non-finite values.
Results may differ from a plain program's by a relative error of at most 0.005.
Values may be sent and summed in bfloat16 or wider, within the bound.
A program may use at most 128 MiB of HBM per device.

v0:
```python
import math

import jax
import jax.numpy as jnp
from jax import lax
from jax.sharding import PartitionSpec as P

GROUP = 16
SPAN = 128


masked_score = -1e30


def shifted(block, axis, distance):
    devices = range(lax.axis_size(axis))
    route = [((i - distance) % len(devices), i) for i in devices]
    return lax.ppermute(block, axis, route)


def locate(span_order, doc_ends, first_row, row_count):
    row_ids = first_row + jnp.arange(row_count, dtype=jnp.int32)
    slot_ids = row_ids // SPAN
    span_ids = jnp.arange(span_order.shape[0], dtype=jnp.int32)
    picked = jnp.sum(
        jnp.where(slot_ids[:, None] == span_ids[None, :], span_order[None, :], 0), axis=1
    )
    positions = picked * SPAN + row_ids % SPAN
    doc_ids = jnp.sum((positions[:, None] >= doc_ends[None, :-1]).astype(jnp.int32), axis=1)
    return (positions, doc_ids)


def attend(online, queries, pair_block, allowed):
    running_max, weight_sum, accumulator = online
    scale = 1.0 / math.sqrt(queries.shape[2])
    scores = (
        jnp.einsum("hqd,kd->hqk", queries, pair_block[0], preferred_element_type=jnp.float32)
        * scale
    )
    scores = jnp.where(allowed[None], scores, masked_score)
    new_max = jnp.maximum(running_max, jnp.max(scores, axis=2))
    factor = jnp.exp(running_max - new_max)
    weights = jnp.where(allowed[None], jnp.exp(scores - new_max[..., None]), 0.0)
    weight_sum = weight_sum * factor + jnp.sum(weights, axis=2)
    mixed = jnp.einsum(
        "hqk,kd->hqd",
        weights.astype(jnp.bfloat16),
        pair_block[1],
        preferred_element_type=jnp.float32,
    )
    accumulator = accumulator * factor[..., None] + mixed
    return (new_max, weight_sum, accumulator)


def body(queries, key_heads, value_heads, doc_lengths, span_order):
    head_count, tok_rows, head_size = queries.shape
    cycle_size = lax.axis_size("ctx")
    self_index = lax.axis_index("ctx")
    group = lax.axis_index("head") * head_count // GROUP
    own_keys = lax.dynamic_index_in_dim(key_heads, group, 0, keepdims=False)
    own_values = lax.dynamic_index_in_dim(value_heads, group, 0, keepdims=False)
    pair_block = jnp.stack([own_keys, own_values])
    doc_ends = jnp.cumsum(doc_lengths)
    query_pos, query_doc = locate(span_order, doc_ends, self_index * tok_rows, tok_rows)

    def absorb(online, block, first_row):
        key_pos, key_doc = locate(span_order, doc_ends, first_row, block.shape[1])
        allowed = (query_doc[:, None] == key_doc[None, :]) & (
            key_pos[None, :] <= query_pos[:, None]
        )
        return attend(online, queries, block, allowed)

    start_state = (
        jnp.full((head_count, tok_rows), masked_score, jnp.float32),
        jnp.zeros((head_count, tok_rows), jnp.float32),
        jnp.zeros((head_count, tok_rows, head_size), jnp.float32),
    )

    def cycle_turn(cycle_step, loop_state):
        online, moving = loop_state
        moving = shifted(moving, "ctx", 1)
        online = absorb(online, moving, (self_index - cycle_step) % cycle_size * tok_rows)
        return (online, moving)

    online = absorb(start_state, pair_block, self_index * tok_rows)
    online, moving = lax.fori_loop(1, cycle_size, cycle_turn, (online, pair_block))
    running_max, weight_sum, accumulator = online
    return (accumulator / weight_sum[..., None]).astype(jnp.bfloat16)


def solution(mesh):
    return jax.shard_map(
        body,
        mesh=mesh,
        in_specs=(P("head", "ctx", None), P(None, "ctx", None), P(None, "ctx", None), P(), P()),
        out_specs=P("head", "ctx", None),
        check_vma=False,
    )
```

profile of v0, /device:TPU:24, one launch (start us, length us, event | category | flops | bytes accessed | tf_op | source)
XLA Modules:
  0.0 329.5 jit_solution(4309051463421755138)
XLA Ops:
  4.0 324.6 %while.22 = (s32[]{:T(128)}, f32[4,256]{1,0:T(4,128)S(1)}, f32[4,256]{1,0:T(4,128)S(1)}, f32[4,256,128]{2,1,0:T(8,128)S(1)}, bf16[2,256,128]{2,1,0:T(8,128)(2,1)...) while((s32[]{:T(128)}, f32[4,256]{1,0:T(4,128)S(1)}, ...), condition=%wide.region_10.11_spmd, body=%wide.region_5.10_spmd.sunk | while | flops 137105680 | bytes 5713542 | solution.py:86
  8.2 11.6 %collective-permute-done = bf16[2,256,128]{2,1,0:T(8,128)(2,1)S(1)} collective-permute-done((bf16[2,256,128]{2,1,0:T(8,128)(2,1)S(1)}, bf16[2,256,128]{2,1,0:T(8,128)(2,1)S(1)}, u32[]{:S(2)}, u32[]{:S(2)}) %collective-permute-start) | collective-permute-done | bytes 131104 | tf_op jit(solution)/shard_map/while/body/eval_jaxpr/ppermute | solution.py:18
  23.2 6.7 %collective-permute-done = bf16[2,256,128]{2,1,0:T(8,128)(2,1)S(1)} collective-permute-done((bf16[2,256,128]{2,1,0:T(8,128)(2,1)S(1)}, bf16[2,256,128]{2,1,0:T(8,128)(2,1)S(1)}, u32[]{:S(2)}, u32[]{:S(2)}) %collective-permute-start) | collective-permute-done | bytes 131104 | tf_op jit(solution)/shard_map/while/body/eval_jaxpr/ppermute | solution.py:18
  33.3 6.7 %collective-permute-done = bf16[2,256,128]{2,1,0:T(8,128)(2,1)S(1)} collective-permute-done((bf16[2,256,128]{2,1,0:T(8,128)(2,1)S(1)}, bf16[2,256,128]{2,1,0:T(8,128)(2,1)S(1)}, u32[]{:S(2)}, u32[]{:S(2)}) %collective-permute-start) | collective-permute-done | bytes 131104 | tf_op jit(solution)/shard_map/while/body/eval_jaxpr/ppermute | solution.py:18
  43.4 6.7 %collective-permute-done = bf16[2,256,128]{2,1,0:T(8,128)(2,1)S(1)} collective-permute-done((bf16[2,256,128]{2,1,0:T(8,128)(2,1)S(1)}, bf16[2,256,128]{2,1,0:T(8,128)(2,1)S(1)}, u32[]{:S(2)}, u32[]{:S(2)}) %collective-permute-start) | collective-permute-done | bytes 131104 | tf_op jit(solution)/shard_map/while/body/eval_jaxpr/ppermute | solution.py:18
  53.5 6.7 %collective-permute-done = bf16[2,256,128]{2,1,0:T(8,128)(2,1)S(1)} collective-permute-done((bf16[2,256,128]{2,1,0:T(8,128)(2,1)S(1)}, bf16[2,256,128]{2,1,0:T(8,128)(2,1)S(1)}, u32[]{:S(2)}, u32[]{:S(2)}) %collective-permute-start) | collective-permute-done | bytes 131104 | tf_op jit(solution)/shard_map/while/body/eval_jaxpr/ppermute | solution.py:18
  63.6 6.7 %collective-permute-done = bf16[2,256,128]{2,1,0:T(8,128)(2,1)S(1)} collective-permute-done((bf16[2,256,128]{2,1,0:T(8,128)(2,1)S(1)}, bf16[2,256,128]{2,1,0:T(8,128)(2,1)S(1)}, u32[]{:S(2)}, u32[]{:S(2)}) %collective-permute-start) | collective-permute-done | bytes 131104 | tf_op jit(solution)/shard_map/while/body/eval_jaxpr/ppermute | solution.py:18
  73.7 6.7 %collective-permute-done = bf16[2,256,128]{2,1,0:T(8,128)(2,1)S(1)} collective-permute-done((bf16[2,256,128]{2,1,0:T(8,128)(2,1)S(1)}, bf16[2,256,128]{2,1,0:T(8,128)(2,1)S(1)}, u32[]{:S(2)}, u32[]{:S(2)}) %collective-permute-start) | collective-permute-done | bytes 131104 | tf_op jit(solution)/shard_map/while/body/eval_jaxpr/ppermute | solution.py:18
  83.8 7.8 %collective-permute-done = bf16[2,256,128]{2,1,0:T(8,128)(2,1)S(1)} collective-permute-done((bf16[2,256,128]{2,1,0:T(8,128)(2,1)S(1)}, bf16[2,256,128]{2,1,0:T(8,128)(2,1)S(1)}, u32[]{:S(2)}, u32[]{:S(2)}) %collective-permute-start) | collective-permute-done | bytes 131104 | tf_op jit(solution)/shard_map/while/body/eval_jaxpr/ppermute | solution.py:18
  95.0 7.2 %collective-permute-done = bf16[2,256,128]{2,1,0:T(8,128)(2,1)S(1)} collective-permute-done((bf16[2,256,128]{2,1,0:T(8,128)(2,1)S(1)}, bf16[2,256,128]{2,1,0:T(8,128)(2,1)S(1)}, u32[]{:S(2)}, u32[]{:S(2)}) %collective-permute-start) | collective-permute-done | bytes 131104 | tf_op jit(solution)/shard_map/while/body/eval_jaxpr/ppermute | solution.py:18
  105.6 6.7 %collective-permute-done = bf16[2,256,128]{2,1,0:T(8,128)(2,1)S(1)} collective-permute-done((bf16[2,256,128]{2,1,0:T(8,128)(2,1)S(1)}, bf16[2,256,128]{2,1,0:T(8,128)(2,1)S(1)}, u32[]{:S(2)}, u32[]{:S(2)}) %collective-permute-start) | collective-permute-done | bytes 131104 | tf_op jit(solution)/shard_map/while/body/eval_jaxpr/ppermute | solution.py:18
  115.7 6.7 %collective-permute-done = bf16[2,256,128]{2,1,0:T(8,128)(2,1)S(1)} collective-permute-done((bf16[2,256,128]{2,1,0:T(8,128)(2,1)S(1)}, bf16[2,256,128]{2,1,0:T(8,128)(2,1)S(1)}, u32[]{:S(2)}, u32[]{:S(2)}) %collective-permute-start) | collective-permute-done | bytes 131104 | tf_op jit(solution)/shard_map/while/body/eval_jaxpr/ppermute | solution.py:18
  125.8 6.7 %collective-permute-done = bf16[2,256,128]{2,1,0:T(8,128)(2,1)S(1)} collective-permute-done((bf16[2,256,128]{2,1,0:T(8,128)(2,1)S(1)}, bf16[2,256,128]{2,1,0:T(8,128)(2,1)S(1)}, u32[]{:S(2)}, u32[]{:S(2)}) %collective-permute-start) | collective-permute-done | bytes 131104 | tf_op jit(solution)/shard_map/while/body/eval_jaxpr/ppermute | solution.py:18
  135.9 6.7 %collective-permute-done = bf16[2,256,128]{2,1,0:T(8,128)(2,1)S(1)} collective-permute-done((bf16[2,256,128]{2,1,0:T(8,128)(2,1)S(1)}, bf16[2,256,128]{2,1,0:T(8,128)(2,1)S(1)}, u32[]{:S(2)}, u32[]{:S(2)}) %collective-permute-start) | collective-permute-done | bytes 131104 | tf_op jit(solution)/shard_map/while/body/eval_jaxpr/ppermute | solution.py:18
  146.0 6.7 %collective-permute-done = bf16[2,256,128]{2,1,0:T(8,128)(2,1)S(1)} collective-permute-done((bf16[2,256,128]{2,1,0:T(8,128)(2,1)S(1)}, bf16[2,256,128]{2,1,0:T(8,128)(2,1)S(1)}, u32[]{:S(2)}, u32[]{:S(2)}) %collective-permute-start) | collective-permute-done | bytes 131104 | tf_op jit(solution)/shard_map/while/body/eval_jaxpr/ppermute | solution.py:18
  156.1 6.7 %collective-permute-done = bf16[2,256,128]{2,1,0:T(8,128)(2,1)S(1)} collective-permute-done((bf16[2,256,128]{2,1,0:T(8,128)(2,1)S(1)}, bf16[2,256,128]{2,1,0:T(8,128)(2,1)S(1)}, u32[]{:S(2)}, u32[]{:S(2)}) %collective-permute-start) | collective-permute-done | bytes 131104 | tf_op jit(solution)/shard_map/while/body/eval_jaxpr/ppermute | solution.py:18
  166.2 7.8 %collective-permute-done = bf16[2,256,128]{2,1,0:T(8,128)(2,1)S(1)} collective-permute-done((bf16[2,256,128]{2,1,0:T(8,128)(2,1)S(1)}, bf16[2,256,128]{2,1,0:T(8,128)(2,1)S(1)}, u32[]{:S(2)}, u32[]{:S(2)}) %collective-permute-start) | collective-permute-done | bytes 131104 | tf_op jit(solution)/shard_map/while/body/eval_jaxpr/ppermute | solution.py:18
  177.4 7.2 %collective-permute-done = bf16[2,256,128]{2,1,0:T(8,128)(2,1)S(1)} collective-permute-done((bf16[2,256,128]{2,1,0:T(8,128)(2,1)S(1)}, bf16[2,256,128]{2,1,0:T(8,128)(2,1)S(1)}, u32[]{:S(2)}, u32[]{:S(2)}) %collective-permute-start) | collective-permute-done | bytes 131104 | tf_op jit(solution)/shard_map/while/body/eval_jaxpr/ppermute | solution.py:18
  188.0 6.7 %collective-permute-done = bf16[2,256,128]{2,1,0:T(8,128)(2,1)S(1)} collective-permute-done((bf16[2,256,128]{2,1,0:T(8,128)(2,1)S(1)}, bf16[2,256,128]{2,1,0:T(8,128)(2,1)S(1)}, u32[]{:S(2)}, u32[]{:S(2)}) %collective-permute-start) | collective-permute-done | bytes 131104 | tf_op jit(solution)/shard_map/while/body/eval_jaxpr/ppermute | solution.py:18
  198.1 6.7 %collective-permute-done = bf16[2,256,128]{2,1,0:T(8,128)(2,1)S(1)} collective-permute-done((bf16[2,256,128]{2,1,0:T(8,128)(2,1)S(1)}, bf16[2,256,128]{2,1,0:T(8,128)(2,1)S(1)}, u32[]{:S(2)}, u32[]{:S(2)}) %collective-permute-start) | collective-permute-done | bytes 131104 | tf_op jit(solution)/shard_map/while/body/eval_jaxpr/ppermute | solution.py:18
  208.2 6.7 %collective-permute-done = bf16[2,256,128]{2,1,0:T(8,128)(2,1)S(1)} collective-permute-done((bf16[2,256,128]{2,1,0:T(8,128)(2,1)S(1)}, bf16[2,256,128]{2,1,0:T(8,128)(2,1)S(1)}, u32[]{:S(2)}, u32[]{:S(2)}) %collective-permute-start) | collective-permute-done | bytes 131104 | tf_op jit(solution)/shard_map/while/body/eval_jaxpr/ppermute | solution.py:18
  218.3 6.7 %collective-permute-done = bf16[2,256,128]{2,1,0:T(8,128)(2,1)S(1)} collective-permute-done((bf16[2,256,128]{2,1,0:T(8,128)(2,1)S(1)}, bf16[2,256,128]{2,1,0:T(8,128)(2,1)S(1)}, u32[]{:S(2)}, u32[]{:S(2)}) %collective-permute-start) | collective-permute-done | bytes 131104 | tf_op jit(solution)/shard_map/while/body/eval_jaxpr/ppermute | solution.py:18
  248.5 7.8 %collective-permute-done = bf16[2,256,128]{2,1,0:T(8,128)(2,1)S(1)} collective-permute-done((bf16[2,256,128]{2,1,0:T(8,128)(2,1)S(1)}, bf16[2,256,128]{2,1,0:T(8,128)(2,1)S(1)}, u32[]{:S(2)}, u32[]{:S(2)}) %collective-permute-start) | collective-permute-done | bytes 131104 | tf_op jit(solution)/shard_map/while/body/eval_jaxpr/ppermute | solution.py:18
  259.8 7.2 %collective-permute-done = bf16[2,256,128]{2,1,0:T(8,128)(2,1)S(1)} collective-permute-done((bf16[2,256,128]{2,1,0:T(8,128)(2,1)S(1)}, bf16[2,256,128]{2,1,0:T(8,128)(2,1)S(1)}, u32[]{:S(2)}, u32[]{:S(2)}) %collective-permute-start) | collective-permute-done | bytes 131104 | tf_op jit(solution)/shard_map/while/body/eval_jaxpr/ppermute | solution.py:18
  (434 shorter events, 163.4 us)
Async XLA Ops:
  4.0 15.8 %collective-permute-start = (bf16[2,256,128]{2,1,0:T(8,128)(2,1)S(1)}, bf16[2,256,128]{2,1,0:T(8,128)(2,1)S(1)}, u32[]{:S(2)}, u32[]{:S(2)}) collective-permute-start(bf16[2,256,128]{2,1,0:T(8,128)(2,1)S(1)} %get-tuple-element.439), channel_id=1, source_target_pairs={{31,0},{0,1},{1,2},{2,3},{3,4},{4,5},{5,6},{6,7},{7,8},{8,9},{9,10... | collective-permute-start | bytes 393224 | tf_op jit(solution)/shard_map/while/body/eval_jaxpr/ppermute | solution.py:18
  20.9 9.0 %collective-permute-start = (bf16[2,256,128]{2,1,0:T(8,128)(2,1)S(1)}, bf16[2,256,128]{2,1,0:T(8,128)(2,1)S(1)}, u32[]{:S(2)}, u32[]{:S(2)}) collective-permute-start(bf16[2,256,128]{2,1,0:T(8,128)(2,1)S(1)} %get-tuple-element.439), channel_id=1, source_target_pairs={{31,0},{0,1},{1,2},{2,3},{3,4},{4,5},{5,6},{6,7},{7,8},{8,9},{9,10... | collective-permute-start | bytes 393224 | tf_op jit(solution)/shard_map/while/body/eval_jaxpr/ppermute | solution.py:18
  31.0 9.0 %collective-permute-start = (bf16[2,256,128]{2,1,0:T(8,128)(2,1)S(1)}, bf16[2,256,128]{2,1,0:T(8,128)(2,1)S(1)}, u32[]{:S(2)}, u32[]{:S(2)}) collective-permute-start(bf16[2,256,128]{2,1,0:T(8,128)(2,1)S(1)} %get-tuple-element.439), channel_id=1, source_target_pairs={{31,0},{0,1},{1,2},{2,3},{3,4},{4,5},{5,6},{6,7},{7,8},{8,9},{9,10... | collective-permute-start | bytes 393224 | tf_op jit(solution)/shard_map/while/body/eval_jaxpr/ppermute | solution.py:18
  41.1 9.0 %collective-permute-start = (bf16[2,256,128]{2,1,0:T(8,128)(2,1)S(1)}, bf16[2,256,128]{2,1,0:T(8,128)(2,1)S(1)}, u32[]{:S(2)}, u32[]{:S(2)}) collective-permute-start(bf16[2,256,128]{2,1,0:T(8,128)(2,1)S(1)} %get-tuple-element.439), channel_id=1, source_target_pairs={{31,0},{0,1},{1,2},{2,3},{3,4},{4,5},{5,6},{6,7},{7,8},{8,9},{9,10... | collective-permute-start | bytes 393224 | tf_op jit(solution)/shard_map/while/body/eval_jaxpr/ppermute | solution.py:18
  51.2 9.0 %collective-permute-start = (bf16[2,256,128]{2,1,0:T(8,128)(2,1)S(1)}, bf16[2,256,128]{2,1,0:T(8,128)(2,1)S(1)}, u32[]{:S(2)}, u32[]{:S(2)}) collective-permute-start(bf16[2,256,128]{2,1,0:T(8,128)(2,1)S(1)} %get-tuple-element.439), channel_id=1, source_target_pairs={{31,0},{0,1},{1,2},{2,3},{3,4},{4,5},{5,6},{6,7},{7,8},{8,9},{9,10... | collective-permute-start | bytes 393224 | tf_op jit(solution)/shard_map/while/body/eval_jaxpr/ppermute | solution.py:18
  61.3 9.0 %collective-permute-start = (bf16[2,256,128]{2,1,0:T(8,128)(2,1)S(1)}, bf16[2,256,128]{2,1,0:T(8,128)(2,1)S(1)}, u32[]{:S(2)}, u32[]{:S(2)}) collective-permute-start(bf16[2,256,128]{2,1,0:T(8,128)(2,1)S(1)} %get-tuple-element.439), channel_id=1, source_target_pairs={{31,0},{0,1},{1,2},{2,3},{3,4},{4,5},{5,6},{6,7},{7,8},{8,9},{9,10... | collective-permute-start | bytes 393224 | tf_op jit(solution)/shard_map/while/body/eval_jaxpr/ppermute | solution.py:18
  71.4 9.0 %collective-permute-start = (bf16[2,256,128]{2,1,0:T(8,128)(2,1)S(1)}, bf16[2,256,128]{2,1,0:T(8,128)(2,1)S(1)}, u32[]{:S(2)}, u32[]{:S(2)}) collective-permute-start(bf16[2,256,128]{2,1,0:T(8,128)(2,1)S(1)} %get-tuple-element.439), channel_id=1, source_target_pairs={{31,0},{0,1},{1,2},{2,3},{3,4},{4,5},{5,6},{6,7},{7,8},{8,9},{9,10... | collective-permute-start | bytes 393224 | tf_op jit(solution)/shard_map/while/body/eval_jaxpr/ppermute | solution.py:18
  81.4 10.1 %collective-permute-start = (bf16[2,256,128]{2,1,0:T(8,128)(2,1)S(1)}, bf16[2,256,128]{2,1,0:T(8,128)(2,1)S(1)}, u32[]{:S(2)}, u32[]{:S(2)}) collective-permute-start(bf16[2,256,128]{2,1,0:T(8,128)(2,1)S(1)} %get-tuple-element.439), channel_id=1, source_target_pairs={{31,0},{0,1},{1,2},{2,3},{3,4},{4,5},{5,6},{6,7},{7,8},{8,9},{9,10... | collective-permute-start | bytes 393224 | tf_op jit(solution)/shard_map/while/body/eval_jaxpr/ppermute | solution.py:18
  92.7 9.5 %collective-permute-start = (bf16[2,256,128]{2,1,0:T(8,128)(2,1)S(1)}, bf16[2,256,128]{2,1,0:T(8,128)(2,1)S(1)}, u32[]{:S(2)}, u32[]{:S(2)}) collective-permute-start(bf16[2,256,128]{2,1,0:T(8,128)(2,1)S(1)} %get-tuple-element.439), channel_id=1, source_target_pairs={{31,0},{0,1},{1,2},{2,3},{3,4},{4,5},{5,6},{6,7},{7,8},{8,9},{9,10... | collective-permute-start | bytes 393224 | tf_op jit(solution)/shard_map/while/body/eval_jaxpr/ppermute | solution.py:18
  103.3 9.0 %collective-permute-start = (bf16[2,256,128]{2,1,0:T(8,128)(2,1)S(1)}, bf16[2,256,128]{2,1,0:T(8,128)(2,1)S(1)}, u32[]{:S(2)}, u32[]{:S(2)}) collective-permute-start(bf16[2,256,128]{2,1,0:T(8,128)(2,1)S(1)} %get-tuple-element.439), channel_id=1, source_target_pairs={{31,0},{0,1},{1,2},{2,3},{3,4},{4,5},{5,6},{6,7},{7,8},{8,9},{9,10... | collective-permute-start | bytes 393224 | tf_op jit(solution)/shard_map/while/body/eval_jaxpr/ppermute | solution.py:18
  113.4 9.0 %collective-permute-start = (bf16[2,256,128]{2,1,0:T(8,128)(2,1)S(1)}, bf16[2,256,128]{2,1,0:T(8,128)(2,1)S(1)}, u32[]{:S(2)}, u32[]{:S(2)}) collective-permute-start(bf16[2,256,128]{2,1,0:T(8,128)(2,1)S(1)} %get-tuple-element.439), channel_id=1, source_target_pairs={{31,0},{0,1},{1,2},{2,3},{3,4},{4,5},{5,6},{6,7},{7,8},{8,9},{9,10... | collective-permute-start | bytes 393224 | tf_op jit(solution)/shard_map/while/body/eval_jaxpr/ppermute | solution.py:18
  123.5 9.0 %collective-permute-start = (bf16[2,256,128]{2,1,0:T(8,128)(2,1)S(1)}, bf16[2,256,128]{2,1,0:T(8,128)(2,1)S(1)}, u32[]{:S(2)}, u32[]{:S(2)}) collective-permute-start(bf16[2,256,128]{2,1,0:T(8,128)(2,1)S(1)} %get-tuple-element.439), channel_id=1, source_target_pairs={{31,0},{0,1},{1,2},{2,3},{3,4},{4,5},{5,6},{6,7},{7,8},{8,9},{9,10... | collective-permute-start | bytes 393224 | tf_op jit(solution)/shard_map/while/body/eval_jaxpr/ppermute | solution.py:18
  163.8 10.1 %collective-permute-start = (bf16[2,256,128]{2,1,0:T(8,128)(2,1)S(1)}, bf16[2,256,128]{2,1,0:T(8,128)(2,1)S(1)}, u32[]{:S(2)}, u32[]{:S(2)}) collective-permute-start(bf16[2,256,128]{2,1,0:T(8,128)(2,1)S(1)} %get-tuple-element.439), channel_id=1, source_target_pairs={{31,0},{0,1},{1,2},{2,3},{3,4},{4,5},{5,6},{6,7},{7,8},{8,9},{9,10... | collective-permute-start | bytes 393224 | tf_op jit(solution)/shard_map/while/body/eval_jaxpr/ppermute | solution.py:18
  175.1 9.5 %collective-permute-start = (bf16[2,256,128]{2,1,0:T(8,128)(2,1)S(1)}, bf16[2,256,128]{2,1,0:T(8,128)(2,1)S(1)}, u32[]{:S(2)}, u32[]{:S(2)}) collective-permute-start(bf16[2,256,128]{2,1,0:T(8,128)(2,1)S(1)} %get-tuple-element.439), channel_id=1, source_target_pairs={{31,0},{0,1},{1,2},{2,3},{3,4},{4,5},{5,6},{6,7},{7,8},{8,9},{9,10... | collective-permute-start | bytes 393224 | tf_op jit(solution)/shard_map/while/body/eval_jaxpr/ppermute | solution.py:18
  185.7 9.0 %collective-permute-start = (bf16[2,256,128]{2,1,0:T(8,128)(2,1)S(1)}, bf16[2,256,128]{2,1,0:T(8,128)(2,1)S(1)}, u32[]{:S(2)}, u32[]{:S(2)}) collective-permute-start(bf16[2,256,128]{2,1,0:T(8,128)(2,1)S(1)} %get-tuple-element.439), channel_id=1, source_target_pairs={{31,0},{0,1},{1,2},{2,3},{3,4},{4,5},{5,6},{6,7},{7,8},{8,9},{9,10... | collective-permute-start | bytes 393224 | tf_op jit(solution)/shard_map/while/body/eval_jaxpr/ppermute | solution.py:18
  195.8 9.0 %collective-permute-start = (bf16[2,256,128]{2,1,0:T(8,128)(2,1)S(1)}, bf16[2,256,128]{2,1,0:T(8,128)(2,1)S(1)}, u32[]{:S(2)}, u32[]{:S(2)}) collective-permute-start(bf16[2,256,128]{2,1,0:T(8,128)(2,1)S(1)} %get-tuple-element.439), channel_id=1, source_target_pairs={{31,0},{0,1},{1,2},{2,3},{3,4},{4,5},{5,6},{6,7},{7,8},{8,9},{9,10... | collective-permute-start | bytes 393224 | tf_op jit(solution)/shard_map/while/body/eval_jaxpr/ppermute | solution.py:18
  205.9 9.0 %collective-permute-start = (bf16[2,256,128]{2,1,0:T(8,128)(2,1)S(1)}, bf16[2,256,128]{2,1,0:T(8,128)(2,1)S(1)}, u32[]{:S(2)}, u32[]{:S(2)}) collective-permute-start(bf16[2,256,128]{2,1,0:T(8,128)(2,1)S(1)} %get-tuple-element.439), channel_id=1, source_target_pairs={{31,0},{0,1},{1,2},{2,3},{3,4},{4,5},{5,6},{6,7},{7,8},{8,9},{9,10... | collective-permute-start | bytes 393224 | tf_op jit(solution)/shard_map/while/body/eval_jaxpr/ppermute | solution.py:18
  216.0 9.0 %collective-permute-start = (bf16[2,256,128]{2,1,0:T(8,128)(2,1)S(1)}, bf16[2,256,128]{2,1,0:T(8,128)(2,1)S(1)}, u32[]{:S(2)}, u32[]{:S(2)}) collective-permute-start(bf16[2,256,128]{2,1,0:T(8,128)(2,1)S(1)} %get-tuple-element.439), channel_id=1, source_target_pairs={{31,0},{0,1},{1,2},{2,3},{3,4},{4,5},{5,6},{6,7},{7,8},{8,9},{9,10... | collective-permute-start | bytes 393224 | tf_op jit(solution)/shard_map/while/body/eval_jaxpr/ppermute | solution.py:18
  246.2 10.1 %collective-permute-start = (bf16[2,256,128]{2,1,0:T(8,128)(2,1)S(1)}, bf16[2,256,128]{2,1,0:T(8,128)(2,1)S(1)}, u32[]{:S(2)}, u32[]{:S(2)}) collective-permute-start(bf16[2,256,128]{2,1,0:T(8,128)(2,1)S(1)} %get-tuple-element.439), channel_id=1, source_target_pairs={{31,0},{0,1},{1,2},{2,3},{3,4},{4,5},{5,6},{6,7},{7,8},{8,9},{9,10... | collective-permute-start | bytes 393224 | tf_op jit(solution)/shard_map/while/body/eval_jaxpr/ppermute | solution.py:18
  257.5 9.5 %collective-permute-start = (bf16[2,256,128]{2,1,0:T(8,128)(2,1)S(1)}, bf16[2,256,128]{2,1,0:T(8,128)(2,1)S(1)}, u32[]{:S(2)}, u32[]{:S(2)}) collective-permute-start(bf16[2,256,128]{2,1,0:T(8,128)(2,1)S(1)} %get-tuple-element.439), channel_id=1, source_target_pairs={{31,0},{0,1},{1,2},{2,3},{3,4},{4,5},{5,6},{6,7},{7,8},{8,9},{9,10... | collective-permute-start | bytes 393224 | tf_op jit(solution)/shard_map/while/body/eval_jaxpr/ppermute | solution.py:18
  268.1 9.0 %collective-permute-start = (bf16[2,256,128]{2,1,0:T(8,128)(2,1)S(1)}, bf16[2,256,128]{2,1,0:T(8,128)(2,1)S(1)}, u32[]{:S(2)}, u32[]{:S(2)}) collective-permute-start(bf16[2,256,128]{2,1,0:T(8,128)(2,1)S(1)} %get-tuple-element.439), channel_id=1, source_target_pairs={{31,0},{0,1},{1,2},{2,3},{3,4},{4,5},{5,6},{6,7},{7,8},{8,9},{9,10... | collective-permute-start | bytes 393224 | tf_op jit(solution)/shard_map/while/body/eval_jaxpr/ppermute | solution.py:18
  278.2 9.0 %collective-permute-start = (bf16[2,256,128]{2,1,0:T(8,128)(2,1)S(1)}, bf16[2,256,128]{2,1,0:T(8,128)(2,1)S(1)}, u32[]{:S(2)}, u32[]{:S(2)}) collective-permute-start(bf16[2,256,128]{2,1,0:T(8,128)(2,1)S(1)} %get-tuple-element.439), channel_id=1, source_target_pairs={{31,0},{0,1},{1,2},{2,3},{3,4},{4,5},{5,6},{6,7},{7,8},{8,9},{9,10... | collective-permute-start | bytes 393224 | tf_op jit(solution)/shard_map/while/body/eval_jaxpr/ppermute | solution.py:18
  288.3 9.0 %collective-permute-start = (bf16[2,256,128]{2,1,0:T(8,128)(2,1)S(1)}, bf16[2,256,128]{2,1,0:T(8,128)(2,1)S(1)}, u32[]{:S(2)}, u32[]{:S(2)}) collective-permute-start(bf16[2,256,128]{2,1,0:T(8,128)(2,1)S(1)} %get-tuple-element.439), channel_id=1, source_target_pairs={{31,0},{0,1},{1,2},{2,3},{3,4},{4,5},{5,6},{6,7},{7,8},{8,9},{9,10... | collective-permute-start | bytes 393224 | tf_op jit(solution)/shard_map/while/body/eval_jaxpr/ppermute | solution.py:18
  298.4 9.0 %collective-permute-start = (bf16[2,256,128]{2,1,0:T(8,128)(2,1)S(1)}, bf16[2,256,128]{2,1,0:T(8,128)(2,1)S(1)}, u32[]{:S(2)}, u32[]{:S(2)}) collective-permute-start(bf16[2,256,128]{2,1,0:T(8,128)(2,1)S(1)} %get-tuple-element.439), channel_id=1, source_target_pairs={{31,0},{0,1},{1,2},{2,3},{3,4},{4,5},{5,6},{6,7},{7,8},{8,9},{9,10... | collective-permute-start | bytes 393224 | tf_op jit(solution)/shard_map/while/body/eval_jaxpr/ppermute | solution.py:18
  (10 other events, 66.9 us)
where the time goes:
time: 331 us; the launch traced here: 330 us
  waiting for transfers between devices  216 us (65%)
  starting transfers between devices  61.4 us (19%)
  matrix products  26.3 us (8%)
  other arithmetic  19.6 us (6%)
    ppermute x31, waiting for transfers between devices, shifted(): return lax.ppermute(block, axis, route)  216 us
    ppermute x31, starting transfers between devices, shifted(): return lax.ppermute(block, axis, route)  61.4 us
    dot_general x32, matrix products, attend(): jnp.einsum('hqk,kd->hqd', weights.astype(jnp.bfloat16), pair_block[1], pr...  16 us
    dot_general x32, matrix products, attend(): jnp.einsum('hqd,kd->hqk', queries, pair_block[0], preferred_element_type=...  10.3 us
    reduce_sum x32, other arithmetic, attend(): weight_sum = weight_sum * factor + jnp.sum(weights, axis=2)  6.65 us
  transfers between devices with their start and end apart: 31, of which 31 were waited for; matrix products, arithmetic and copies ran while one was open for 3% of the time, Pallas kernels for 0%

commit v1 on v0

v1 whole, which is shorter than its diff:
```python
import math

import jax
import jax.numpy as jnp
from jax import lax
from jax.experimental import pallas as pl
from jax.experimental.pallas import tpu as pltpu
from jax.sharding import PartitionSpec as P

MESH = pl.DeviceIdType.MESH
SPAN = 128
DH = 128
DOCS = 16
SPANS = 64
RING = 16
BIG = 131072.0
FACTOR = math.log2(math.e) / math.sqrt(DH)
ONES = 16
COMM = True
COMPUTE = True


def kernel(q_ref, k_ref, v_ref, lens_ref, order_ref, out_ref,
           buf, ext, qx, vtmp, acc, top, send_sem, recv_sem, local_sem):
    head = lax.axis_index("head")
    ctx = lax.axis_index("ctx")
    core = lax.rem(head, 2)
    y_lo = lax.rem(head // 2, 2)
    x_lo = ctx // RING
    z = lax.rem(ctx, RING)
    group = head // 4

    own = 2 * ctx
    local = [
        pltpu.make_async_copy(k_ref.at[group], buf.at[0, pl.ds(own, 2)], local_sem.at[0]),
        pltpu.make_async_copy(v_ref.at[group], vtmp, local_sem.at[1]),
        pltpu.make_async_copy(q_ref, qx.at[:, :, pl.ds(0, DH)], local_sem.at[2]),
    ]
    for copy in local:
        copy.start()

    other_x = 1 - x_lo
    to_up = {"ctx": x_lo * RING + lax.rem(z + 1, RING)}
    to_down = {"ctx": x_lo * RING + lax.rem(z + RING - 1, RING)}
    to_x = {"ctx": other_x * RING + z}
    to_y = {"head": head + 2 - 4 * y_lo}
    to_core = {"head": head + 1 - 2 * core}

    if COMM:
        barrier = pltpu.get_barrier_semaphore()
        for device in (to_up, to_down, to_x, to_y, to_core):
            pl.semaphore_signal(barrier, inc=1, device_id=device, device_id_type=MESH)

    def unit(kv, span, device):
        return pltpu.make_async_remote_copy(
            src_ref=buf.at[kv, span],
            dst_ref=buf.at[kv, span],
            send_sem=send_sem,
            recv_sem=recv_sem.at[kv, span],
            device_id=device,
            device_id_type=MESH,
        )

    def send(kv, span, device):
        if COMM:
            unit(kv, span, device).start()

    def arrived(kv, span):
        if COMM:
            unit(kv, span, to_core).wait_recv()

    def first(x, level, side):
        return 2 * (x * RING + lax.rem(level + RING, RING)) + (y_lo if side == 0 else 1 - y_lo)

    def along(t, side, directions, onward):
        for direction in directions:
            span = first(x_lo, z - direction * t, side)
            arrived(core, span)
            if direction in onward:
                send(core, span, to_up if direction == 1 else to_down)
            if side == 0:
                send(core, span, to_x)
            send(core, span, to_core)

    def levels(t):
        return [z - t, z + t]

    def from_x(places):
        for level in places:
            span = first(other_x, level, 0)
            arrived(core, span)
            send(core, span, to_y)
            send(core, span, to_core)

    def from_y(places):
        for level in places:
            span = first(other_x, level, 1)
            arrived(core, span)
            send(core, span, to_core)

    def ready(x, places):
        for level in places:
            for side in (0, 1):
                arrived(1 - core, first(x, level, side))

    def attend(slots, own_slot=False):
        if not COMPUTE:
            return
        spans = [2 * (x * RING + lax.rem(level + RING, RING)) + j for x, level in slots for j in (0, 1)]
        keys = jnp.concatenate(
            [jnp.concatenate([buf[0, s], ext[s]], axis=1) for s in spans], axis=0
        )
        values = jnp.concatenate([buf[1, s] for s in spans], axis=1)
        values = jnp.concatenate(
            [values, jnp.ones((ONES, values.shape[1]), jnp.bfloat16)], axis=0
        )
        for h in range(4):
            scores = lax.dot_general(
                keys, qx[h], (((1,), (1,)), ((), ())), preferred_element_type=jnp.float32
            )
            if own_slot:
                key_row = lax.broadcasted_iota(jnp.int32, scores.shape, 0)
                query_row = lax.broadcasted_iota(jnp.int32, scores.shape, 1)
                later = (key_row > query_row) & (
                    (key_row >= SPAN) == (query_row >= SPAN)
                )
                scores = jnp.where(later, -BIG, scores)
            scores = scores * FACTOR
            highest = jnp.max(scores, axis=0, keepdims=True)
            if own_slot:
                new_top = highest
            else:
                old_top = top[h:h + 1, :]
                new_top = jnp.maximum(old_top, highest)
            weights = jnp.exp2(scores - new_top).astype(jnp.bfloat16)
            mixed = lax.dot_general(
                values, weights, (((1,), (0,)), ((), ())), preferred_element_type=jnp.float32
            )
            if own_slot:
                acc[h] = mixed
            else:
                acc[h] = acc[h] * jnp.exp2(old_top - new_top) + mixed
            top[h:h + 1, :] = new_top

    local[1].wait()
    for j in (0, 1):
        block = vtmp[j * SPAN:(j + 1) * SPAN, :].astype(jnp.float32)
        buf[1, own + j] = block.T.astype(jnp.bfloat16)
    local[0].wait()
    if COMM:
        pl.semaphore_wait(barrier, 5)
    for side in (0, 1):
        span = first(x_lo, z, side)
        send(core, span, to_up)
        send(core, span, to_down)
        if side == 0:
            send(core, span, to_x)

    lane = lax.broadcasted_iota(jnp.int32, (1, DH), 1)
    opens = jnp.where(lane < SPANS, lane * SPAN, 1 << 20)
    closes = jnp.where(lane < SPANS, lane * SPAN + SPAN, 1 << 20)
    end = jnp.int32(0)
    for d in range(DOCS):
        opens = jnp.where(lane == SPANS + d, end, opens)
        end = end + lens_ref[d]
        closes = jnp.where(lane == SPANS + d, end if d < DOCS - 1 else 1 << 20, closes)

    def inside(span):
        position = order_ref[span] * SPAN + lax.broadcasted_iota(jnp.int32, (SPAN, 1), 0)
        return (position >= opens) & (position < closes)

    def marks(s, carry):
        ext[s] = jnp.where(inside(s), 1.0, 0.0).astype(jnp.bfloat16)
        return carry

    for j in (0, 1):
        outside = jnp.where(inside(own + j), 0.0, -BIG)
        after = jnp.where(lane > order_ref[own + j], -BIG, 0.0)
        side_q = jnp.where(lane < SPANS, after, jnp.where(lane < SPANS + DOCS, outside, 0.0))
        for h in range(4):
            qx[h, j * SPAN:(j + 1) * SPAN, DH:] = side_q.astype(jnp.bfloat16)
    lax.fori_loop(0, SPANS, marks, 0, unroll=4)
    local[2].wait()

    along(1, 0, (1, -1), (1, -1))
    along(1, 1, (1, -1), (1, -1))
    attend([(x_lo, z)], own_slot=True)

    def turn(t, carry):
        @pl.when(t <= 6)
        def _():
            along(t, 0, (1, -1), (1, -1))

        @pl.when(t == 7)
        def _():
            along(t, 0, (1, -1), (1,))

        @pl.when(t == 8)
        def _():
            along(t, 0, (1,), ())

        @pl.when(t <= 8)
        def _():
            from_x(levels(t - 1))
            ready(x_lo, levels(t - 1))
            attend([(x_lo, level) for level in levels(t - 1)])

        @pl.when(t <= 6)
        def _():
            along(t, 1, (1, -1), (1, -1))

        @pl.when(t == 7)
        def _():
            along(t, 1, (1, -1), (-1,))

        @pl.when(t == 8)
        def _():
            along(t, 1, (-1,), ())

        @pl.when(t == 9)
        def _():
            from_x([z - 8])

        @pl.when((t >= 3) & (t <= 9))
        def _():
            from_y(levels(t - 2))

        @pl.when(t == 10)
        def _():
            from_y([z - 8])

        @pl.when(t >= 4)
        def _():
            ready(other_x, levels(t - 3))
            attend([(other_x, level) for level in levels(t - 3)])

        @pl.when(t == 2)
        def _():
            from_x([z])

        @pl.when(t == 3)
        def _():
            from_y([z])
            ready(other_x, [z])
            attend([(other_x, z)])

        return carry

    lax.fori_loop(2, 11, turn, 0)
    ready(x_lo, [z - 8])
    ready(other_x, [z - 8])
    attend([(x_lo, z - 8), (other_x, z - 8)])

    if COMPUTE:
        for h in range(4):
            result = acc[h, :DH, :] / acc[h, DH:DH + 1, :]
            out_ref[h] = result.T.astype(jnp.bfloat16)
    else:
        for h in range(4):
            out_ref[h] = (buf[0, 2 * h].astype(jnp.float32) + buf[1, 2 * h + 9]).astype(jnp.bfloat16)[:1, :] + jnp.zeros((256, DH), jnp.bfloat16)
    if COMM:
        pltpu.make_async_copy(buf.at[:, pl.ds(0, 62)], buf.at[:, pl.ds(0, 62)], send_sem).wait()


def body(queries, key_heads, value_heads, doc_lengths, span_order):
    heads, rows, _ = queries.shape
    shape = (key_heads.shape[0], 2, SPAN, DH)
    return pl.pallas_call(
        kernel,
        out_shape=jax.ShapeDtypeStruct(queries.shape, jnp.bfloat16),
        in_specs=[
            pl.BlockSpec(memory_space=pl.ANY),
            pl.BlockSpec(memory_space=pl.ANY),
            pl.BlockSpec(memory_space=pl.ANY),
            pl.BlockSpec(memory_space=pltpu.SMEM),
            pl.BlockSpec(memory_space=pltpu.SMEM),
        ],
        out_specs=pl.BlockSpec(memory_space=pltpu.VMEM),
        scratch_shapes=[
            pltpu.VMEM((2, SPANS, SPAN, DH), jnp.bfloat16),
            pltpu.VMEM((SPANS, SPAN, DH), jnp.bfloat16),
            pltpu.VMEM((heads, rows, 2 * DH), jnp.bfloat16),
            pltpu.VMEM((rows, DH), jnp.bfloat16),
            pltpu.VMEM((heads, DH + ONES, rows), jnp.float32),
            pltpu.VMEM((8, rows), jnp.float32),
            pltpu.SemaphoreType.DMA,
            pltpu.SemaphoreType.DMA((2, SPANS)),
            pltpu.SemaphoreType.DMA((3,)),
        ],
        compiler_params=pltpu.CompilerParams(
            collective_id=0 if COMM else None, has_side_effects=True, vmem_limit_bytes=48 * 2**20
        ),
        cost_estimate=pl.CostEstimate(
            flops=4 * heads * rows * SPANS * SPAN * DH,
            bytes_accessed=2**20,
            transcendentals=heads * rows * SPANS * SPAN,
        ),
    )(queries, key_heads.reshape(shape), value_heads, doc_lengths, span_order)


def solution(mesh):
    return jax.shard_map(
        body,
        mesh=mesh,
        in_specs=(P("head", "ctx", None), P(None, "ctx", None), P(None, "ctx", None), P(), P()),
        out_specs=P("head", "ctx", None),
        check_vma=False,
    )
```

time: 331 us -> 55.5 us (0.17)
  the two profiles are of different devices: /device:TPU:24 before, /device:TPU:1 now
where the time goes in v1:
time: 55.5 us; the launch traced here: 55.3 us
  Pallas kernels  51 us (92%)
  local copies, waits for them, and re-layouts  4.22 us (8%)
    pallas_call x1, Pallas kernels, body(): pl.pallas_call(kernel, out_shape=jax.ShapeDtypeStruct(queries.shape, jnp....  51 us
    unnamed x11, local copies, waits for them, and re-layouts  4.22 us

profile of v1, /device:TPU:1, one launch (start us, length us, event | category | flops | bytes accessed | tf_op | source)
XLA Modules:
  0.0 55.3 jit_solution(9826321501028344672)
XLA Ops:
  0.0 0.0 copy-start.4
  0.0 0.0 copy-start.3
  0.0 0.7 %copy-done.4 = s32[64]{0:T(128)S(1)} copy-done((s32[64]{0:T(128)S(1)}, s32[64]{0:T(128)}, u32[]{:S(2)}) %copy-start.4) | copy-done | bytes 280
  0.7 0.0 copy-done.3
  0.7 0.0 copy-start
  0.7 0.9 %copy-done = bf16[4,256,128]{2,1,0:T(8,128)(2,1)S(1)} copy-done((bf16[4,256,128]{2,1,0:T(8,128)(2,1)S(1)}, bf16[4,256,128]{2,1,0:T(8,128)(2,1)}, u32[]{:S(2)}) %copy-start) | copy-done | bytes 262168
  1.6 0.0 copy-start.1
  1.6 0.9 %copy-done.1 = bf16[4,256,128]{2,1,0:T(8,128)(2,1)S(1)} copy-done((bf16[4,256,128]{2,1,0:T(8,128)(2,1)S(1)}, bf16[4,256,128]{2,1,0:T(8,128)(2,1)}, u32[]{:S(2)}) %copy-start.1) | copy-done | bytes 262168
  2.6 0.0 copy-start.2
  2.6 0.9 %copy-done.2 = bf16[4,256,128]{2,1,0:T(8,128)(2,1)S(1)} copy-done((bf16[4,256,128]{2,1,0:T(8,128)(2,1)S(1)}, bf16[4,256,128]{2,1,0:T(8,128)(2,1)}, u32[]{:S(2)}) %copy-start.2) | copy-done | bytes 262168
  3.5 51.0 %shard_map.55 = bf16[4,256,128]{2,1,0:T(8,128)(2,1)S(1)} custom-call(bf16[4,256,128]{2,1,0:T(8,128)(2,1)S(1)} %copy-done, bf16[4,2,128,128]{3,2,1,0:T(8,128)(2,1)S(1)} %bitcast.1, bf16[4,256,128]{2,1,0:T(8,128)(2,1)S(1)} %copy-done.2, s32[16]{0:T(128)S(1)} %copy-done.3, s32[64]{0:T(128)S(1)} %copy-done.4), custom_call_target="tpu_custom_call" | custom-call | flops 4294967296 | bytes 1048576 | tf_op jit(solution)/shard_map/pallas_call | solution.py:268
  54.6 0.7 %copy.7 = bf16[4,256,128]{2,1,0:T(8,128)(2,1)} copy(bf16[4,256,128]{2,1,0:T(8,128)(2,1)S(1)} %shard_map.55) | data formatting | bytes 524288
Async XLA Ops:
  0.0 0.7 %copy-start.4 = (s32[64]{0:T(128)S(1)}, s32[64]{0:T(128)}, u32[]{:S(2)}) copy-start(s32[64]{0:T(128)} %order_ref.1) | copy-start | bytes 772
  0.0 0.7 %copy-start.3 = (s32[16]{0:T(128)S(1)}, s32[16]{0:T(128)}, u32[]{:S(2)}) copy-start(s32[16]{0:T(128)} %lens_ref.1) | copy-start | bytes 196
  0.7 0.9 %copy-start = (bf16[4,256,128]{2,1,0:T(8,128)(2,1)S(1)}, bf16[4,256,128]{2,1,0:T(8,128)(2,1)}, u32[]{:S(2)}) copy-start(bf16[4,256,128]{2,1,0:T(8,128)(2,1)} %q_ref.1) | copy-start | bytes 786436
  1.6 0.9 %copy-start.1 = (bf16[4,256,128]{2,1,0:T(8,128)(2,1)S(1)}, bf16[4,256,128]{2,1,0:T(8,128)(2,1)}, u32[]{:S(2)}) copy-start(bf16[4,256,128]{2,1,0:T(8,128)(2,1)} %param.6) | copy-start | bytes 786436
  2.6 0.9 %copy-start.2 = (bf16[4,256,128]{2,1,0:T(8,128)(2,1)S(1)}, bf16[4,256,128]{2,1,0:T(8,128)(2,1)}, u32[]{:S(2)}) copy-start(bf16[4,256,128]{2,1,0:T(8,128)(2,1)} %v_ref.1) | copy-start | bytes 786436

commit v2 on v1

v2 whole, which is shorter than its diff:
```python
import math

import jax
import jax.numpy as jnp
from jax import lax
from jax.experimental import pallas as pl
from jax.experimental.pallas import tpu as pltpu
from jax.sharding import PartitionSpec as P

MESH = pl.DeviceIdType.MESH
SPAN = 128
DH = 128
DOCS = 16
SPANS = 64
RING = 16
BIG = 131072.0
FACTOR = math.log2(math.e) / math.sqrt(DH)
ONES = 16
COMM = True
COMPUTE = True


def kernel(q_ref, k_ref, v_ref, lens_ref, order_ref, out_ref,
           buf, ext, qx, qtmp, vtmp, acc, top, send_sem, recv_sem, local_sem):
    head = lax.axis_index("head")
    ctx = lax.axis_index("ctx")
    core = lax.rem(head, 2)
    y_lo = lax.rem(head // 2, 2)
    x_lo = ctx // RING
    z = lax.rem(ctx, RING)
    group = head // 4
    own = 2 * ctx
    other_x = 1 - x_lo

    local = [
        pltpu.make_async_copy(k_ref.at[group], buf.at[0, pl.ds(own, 2)], local_sem.at[0]),
        pltpu.make_async_copy(v_ref.at[group], vtmp, local_sem.at[1]),
        pltpu.make_async_copy(q_ref, qtmp, local_sem.at[2]),
    ]
    for copy in local:
        copy.start()

    def along(distance):
        return {"ctx": x_lo * RING + lax.rem(z + distance + RING, RING)}

    to_x = {"ctx": other_x * RING + z}
    to_y = {"head": head + 2 - 4 * y_lo}
    to_core = {"head": head + 1 - 2 * core}

    if COMM:
        barrier = pltpu.get_barrier_semaphore()
        for device in (along(1), along(-1), along(2), along(-2), to_x, to_y, to_core):
            pl.semaphore_signal(barrier, inc=1, device_id=device, device_id_type=MESH)

    def unit(kv, span, device):
        return pltpu.make_async_remote_copy(
            src_ref=buf.at[kv, span],
            dst_ref=buf.at[kv, span],
            send_sem=send_sem,
            recv_sem=recv_sem.at[kv, span],
            device_id=device,
            device_id_type=MESH,
        )

    def send(span, device):
        if COMM:
            unit(core, span, device).start()

    def arrived(kv, span):
        if COMM:
            unit(kv, span, to_core).wait_recv()

    def place(x, distance):
        return x * RING + lax.rem(z + distance + RING, RING)

    def span_of(slot, side):
        return 2 * slot + (y_lo if side == 0 else 1 - y_lo)

    def relay(x, distance, side, *devices):
        span = span_of(place(x, distance), side)
        arrived(core, span)
        for device in devices:
            send(span, device)
        send(span, to_core)

    def z_even(e):
        for way in (1, -1):
            for side in (0, 1):
                devices = []
                if e < 3:
                    devices.append(along(2 * way))
                if e == 3 and side == 0 and way == 1:
                    devices.append(along(2))
                if side == 0:
                    devices.append(along(way))
                if side == 0 or e < 3:
                    devices.append(to_x)
                relay(x_lo, -way * 2 * e, side, *devices)

    def z_leaf(e):
        for way in (1, -1):
            relay(x_lo, -way * (2 * e - 1), 0, to_y, to_x)

    def z_part(e):
        if e < 4:
            z_even(e)
        else:
            relay(x_lo, -8, 0, to_y, to_x)
        z_leaf(e)

    def y_own(e):
        for way in (1, -1):
            relay(x_lo, -way * (2 * e - 1), 1)
        if e == 4:
            relay(x_lo, -8, 1)

    def x_part(e):
        if e == 0:
            relay(other_x, 0, 0)
            relay(other_x, 0, 1)
            return
        if e == 4:
            relay(other_x, -8, 0, to_y)
        for way in (1, -1):
            relay(other_x, -way * (2 * e - 1), 0, to_y)
        if e < 4:
            for way in (1, -1):
                if e < 3:
                    relay(other_x, -way * 2 * e, 0)
                    relay(other_x, -way * 2 * e, 1)
                else:
                    relay(other_x, -way * 2 * e, 0, to_y)

    def y_other(e):
        if e == 4:
            relay(other_x, -8, 1)
        for way in (1, -1):
            relay(other_x, -way * (2 * e - 1), 1)
        if e == 3:
            for way in (1, -1):
                relay(other_x, -way * 2 * e, 1)

    def ready(slot):
        for side in (0, 1):
            arrived(1 - core, span_of(slot, side))

    def attend(slots, own_slot=False):
        if not COMPUTE:
            return
        spans = [2 * slot + j for slot in slots for j in (0, 1)]
        keys = jnp.concatenate(
            [jnp.concatenate([buf[0, s], ext[s]], axis=1) for s in spans], axis=0
        )
        values = jnp.concatenate([buf[1, s] for s in spans], axis=1)
        values = jnp.concatenate(
            [values, jnp.ones((ONES, values.shape[1]), jnp.bfloat16)], axis=0
        )
        scores = jnp.dot(keys, qx[...], preferred_element_type=jnp.float32)
        if own_slot:
            key_row = lax.broadcasted_iota(jnp.int32, scores.shape, 0)
            query_row = lax.broadcasted_iota(jnp.int32, scores.shape, 1) % (2 * SPAN)
            later = (key_row > query_row) & ((key_row >= SPAN) == (query_row >= SPAN))
            scores = jnp.where(later, -BIG, scores)
        scores = scores * FACTOR
        highest = jnp.max(scores, axis=0, keepdims=True)
        if own_slot:
            new_top = highest
        else:
            old_top = top[0:1, :]
            new_top = jnp.maximum(old_top, highest)
        weights = jnp.exp2(scores - new_top).astype(jnp.bfloat16)
        mixed = jnp.dot(values, weights, preferred_element_type=jnp.float32)
        if own_slot:
            acc[...] = mixed
        else:
            acc[...] = acc[...] * jnp.exp2(old_top - new_top) + mixed
        top[0:1, :] = new_top

    local[1].wait()
    for j in (0, 1):
        block = vtmp[j * SPAN:(j + 1) * SPAN, :].astype(jnp.float32)
        buf[1, own + j] = block.T.astype(jnp.bfloat16)
    local[0].wait()
    if COMM:
        pl.semaphore_wait(barrier, 7)
    mine = [span_of(ctx, side) for side in (0, 1)]
    for device in (along(2), along(-2)):
        send(mine[0], device)
    for device in (along(2), along(-2)):
        send(mine[1], device)
    for device in (along(1), along(-1), to_x):
        send(mine[0], device)
    send(mine[1], to_x)

    def borders(lane):
        opens = jnp.where(lane < SPANS, lane * SPAN, 1 << 20)
        closes = jnp.where(lane < SPANS, lane * SPAN + SPAN, 1 << 20)
        end = jnp.int32(0)
        for d in range(DOCS):
            opens = jnp.where(lane == SPANS + d, end, opens)
            end = end + lens_ref[d]
            closes = jnp.where(lane == SPANS + d, end if d < DOCS - 1 else 1 << 20, closes)
        return opens, closes

    lane = lax.broadcasted_iota(jnp.int32, (1, DH), 1)
    opens, closes = borders(lane)
    row = lax.broadcasted_iota(jnp.int32, (DH, 1), 0)
    row_opens, row_closes = borders(row)

    def marks(s, carry):
        position = order_ref[s] * SPAN + lax.broadcasted_iota(jnp.int32, (SPAN, 1), 0)
        inside = (position >= opens) & (position < closes)
        ext[s] = jnp.where(inside, 1.0, 0.0).astype(jnp.bfloat16)
        return carry

    empty = jnp.where(lane == SPANS + DOCS, 1.0, 0.0) + jnp.zeros((SPAN, 1), jnp.float32)
    for j in (0, 1):
        ext[SPANS + j] = empty.astype(jnp.bfloat16)
        buf[0, SPANS + j] = jnp.zeros((SPAN, DH), jnp.bfloat16)
        buf[1, SPANS + j] = jnp.zeros((SPAN, DH), jnp.bfloat16)
        position = order_ref[own + j] * SPAN + lax.broadcasted_iota(jnp.int32, (1, SPAN), 1)
        outside = jnp.where((position >= row_opens) & (position < row_closes), 0.0, -BIG)
        after = jnp.where(row > order_ref[own + j], -BIG, 0.0) + jnp.zeros((1, SPAN), jnp.float32)
        last = jnp.where(row == SPANS + DOCS, -BIG, 0.0) + jnp.zeros((1, SPAN), jnp.float32)
        side_q = jnp.where(row < SPANS, after, jnp.where(row < SPANS + DOCS, outside, last))
        for h in range(4):
            qx[DH:, (2 * h + j) * SPAN:(2 * h + j + 1) * SPAN] = side_q.astype(jnp.bfloat16)
    lax.fori_loop(0, SPANS, marks, 0, unroll=4)
    local[2].wait()
    for h in range(4):
        qx[:DH, 2 * h * SPAN:2 * (h + 1) * SPAN] = (
            qtmp[h].astype(jnp.float32).T.astype(jnp.bfloat16)
        )

    attend([ctx], own_slot=True)
    x_part(0)
    z_part(1)

    parts = {
        1: [(y_own, 1), (z_part, 2), (x_part, 1)],
        2: [(y_other, 1), (y_own, 2), (z_part, 3)],
        3: [(x_part, 2)],
        4: [(z_part, 4), (y_own, 3), (y_other, 2)],
        5: [(x_part, 3)],
        6: [(y_own, 4), (x_part, 4), (y_other, 3)],
        7: [(y_other, 4)],
        8: [],
    }

    def turn(i, carry):
        for k, steps in parts.items():
            if steps:
                @pl.when(i == k)
                def _():
                    for step, e in steps:
                        step(e)

        far = 1 - lax.rem(i, 2)
        e = (i + 1) // 2
        last = e // 4
        x = x_lo * (1 - far) + other_x * far
        slots = [place(x, 1 - 2 * e), place(x, 2 * e - 1), place(x, -2 * e)]
        special = far * (SPANS // 2) + (1 - far) * (other_x * RING + z)
        slots.append(place(x, 2 * e) * (1 - last) + special * last)
        for slot in slots[:3]:
            ready(slot)

        @pl.when(i < 8)
        def _():
            ready(slots[3])

        attend(slots)
        return carry

    lax.fori_loop(1, 9, turn, 0)

    if COMPUTE:
        result = acc[:DH, :] / acc[DH:DH + 1, :]
        for h in range(4):
            out_ref[h] = result[:, 2 * h * SPAN:2 * (h + 1) * SPAN].T.astype(jnp.bfloat16)
    else:
        for h in range(4):
            out_ref[h] = (buf[0, 2 * h].astype(jnp.float32) + buf[1, 2 * h + 9]).astype(jnp.bfloat16)[:1, :] + jnp.zeros((256, DH), jnp.bfloat16)
    if COMM:
        pltpu.make_async_copy(buf.at[:, pl.ds(0, 62)], buf.at[:, pl.ds(0, 62)], send_sem).wait()


def body(queries, key_heads, value_heads, doc_lengths, span_order):
    heads, rows, _ = queries.shape
    shape = (key_heads.shape[0], 2, SPAN, DH)
    return pl.pallas_call(
        kernel,
        out_shape=jax.ShapeDtypeStruct(queries.shape, jnp.bfloat16),
        in_specs=[
            pl.BlockSpec(memory_space=pl.ANY),
            pl.BlockSpec(memory_space=pl.ANY),
            pl.BlockSpec(memory_space=pl.ANY),
            pl.BlockSpec(memory_space=pltpu.SMEM),
            pl.BlockSpec(memory_space=pltpu.SMEM),
        ],
        out_specs=pl.BlockSpec(memory_space=pltpu.VMEM),
        scratch_shapes=[
            pltpu.VMEM((2, SPANS + 2, SPAN, DH), jnp.bfloat16),
            pltpu.VMEM((SPANS + 2, SPAN, DH), jnp.bfloat16),
            pltpu.VMEM((2 * DH, heads * rows), jnp.bfloat16),
            pltpu.VMEM((heads, rows, DH), jnp.bfloat16),
            pltpu.VMEM((rows, DH), jnp.bfloat16),
            pltpu.VMEM((DH + ONES, heads * rows), jnp.float32),
            pltpu.VMEM((8, heads * rows), jnp.float32),
            pltpu.SemaphoreType.DMA,
            pltpu.SemaphoreType.DMA((2, SPANS)),
            pltpu.SemaphoreType.DMA((3,)),
        ],
        compiler_params=pltpu.CompilerParams(
            collective_id=0 if COMM else None, has_side_effects=True, vmem_limit_bytes=62 * 2**20
        ),
        cost_estimate=pl.CostEstimate(
            flops=4 * heads * rows * SPANS * SPAN * DH,
            bytes_accessed=2**20,
            transcendentals=heads * rows * SPANS * SPAN,
        ),
    )(queries, key_heads.reshape(shape), value_heads, doc_lengths, span_order)


def solution(mesh):
    return jax.shard_map(
        body,
        mesh=mesh,
        in_specs=(P("head", "ctx", None), P(None, "ctx", None), P(None, "ctx", None), P(), P()),
        out_specs=P("head", "ctx", None),
        check_vma=False,
    )
```

time: 55.5 us -> 51.5 us (0.928)
  local copies, waits for them, and re-layouts: 4.22 us -> 1.67 us
  Pallas kernels: 51 us -> 49.6 us
    unnamed x11 -> x1, local copies, waits for them, and re-layouts: 4.22 us -> 1.67 us
    pallas_call x1, Pallas kernels: 51 us -> 49.6 us  [body(): pl.pallas_call(kernel, out_shape=jax.ShapeDtypeStruct(queries.shape, jnp....]
where the time goes in v2:
time: 51.5 us; the launch traced here: 51.3 us
  Pallas kernels  49.6 us (96%)
  local copies, waits for them, and re-layouts  1.67 us (3%)
    pallas_call x1, Pallas kernels, body(): pl.pallas_call(kernel, out_shape=jax.ShapeDtypeStruct(queries.shape, jnp....  49.6 us
    unnamed x1, local copies, waits for them, and re-layouts  1.67 us

profile of v2, /device:TPU:1, one launch (start us, length us, event | category | flops | bytes accessed | tf_op | source)
XLA Modules:
  0.0 51.3 jit_solution(16563923957062806614)
XLA Ops:
  0.0 49.6 %shard_map.55 = bf16[4,256,128]{2,1,0:T(8,128)(2,1)} custom-call(bf16[4,256,128]{2,1,0:T(8,128)(2,1)} %q_ref.1, bf16[4,2,128,128]{3,2,1,0:T(8,128)(2,1)} %bitcast.1, bf16[4,256,128]{2,1,0:T(8,128)(2,1)} %v_ref.1, s32[16]{0:T(128)} %lens_ref.1, s32[64]{0:T(128)} %order_ref.1), custom_call_target="tpu_custom_call" | custom-call | flops 4294967296 | bytes 1048576 | tf_op jit(solution)/shard_map/pallas_call | solution.py:291
  49.6 1.7 %copy.7 = bf16[4,256,128]{2,1,0:T(8,128)(2,1)} copy(bf16[4,256,128]{2,1,0:T(8,128)(2,1)} %shard_map.55) | data formatting | bytes 524288

commit v3 on v2

v3 whole, which is shorter than its diff:
```python
import math

import jax
import jax.numpy as jnp
from jax import lax
from jax.experimental import pallas as pl
from jax.experimental.pallas import tpu as pltpu
from jax.sharding import PartitionSpec as P

MESH = pl.DeviceIdType.MESH
SPAN = 128
DH = 128
DOCS = 16
SPANS = 64
RING = 16
BIG = 131072.0
FACTOR = math.log2(math.e) / math.sqrt(DH)
ONES = 16
COMM = True
COMPUTE = True


PAIRS = [
    (("A", 1), ("A", -1)), (("A", 3), ("A", -3)),
    (("A", 2), ("A", -2)), (("B", 1), ("B", -1)),
    (("B", 3), ("B", -3)), (("A", 6), ("A", -6)),
    (("B", 2), ("B", -2)), (("A", 5), ("A", -5)),
    (("A", 4), ("A", -4)), (("A", 8), ("B", 0)),
    (("B", 6), ("B", -6)), (("A", 7), ("A", -7)),
    (("B", 5), ("B", -5)), (("B", 8), None),
    (("B", 4), ("B", -4)), (("B", 7), ("B", -7)),
]
PLACE = {}
for _n, _pair in enumerate(PAIRS):
    for _m, _slot in enumerate(_pair):
        for _side in (0, 1):
            PLACE[_slot, _side] = 4 * _n + 2 * _side + _m
PLACE[("A", 0), 0] = 64
PLACE[("A", 0), 1] = 65
OVER_X = (1, 4, 5, 6)
ORDER = [
    [("B", 0, 0), ("B", 0, 1), ("A", 3, 0), ("A", 2, 0), ("A", 1, 0), ("A", 1, 1),
     ("A", 3, 1), ("B", 3, 0), ("A", 6, 0)],
    [("A", 2, 1), ("B", 2, 0), ("A", 5, 0), ("A", 4, 0), ("B", 1, 0), ("B", 1, 1),
     ("B", 3, 1), ("A", 8, 0), ("A", 7, 0)],
    [("B", 6, 0), ("A", 6, 1), ("B", 5, 0)],
    [("B", 2, 1), ("B", 4, 0), ("A", 5, 1), ("B", 8, 0)],
    [("A", 4, 1), ("B", 7, 0), ("A", 8, 1)],
    [("B", 6, 1), ("A", 7, 1), ("B", 8, 1), ("B", 5, 1)],
    [("B", 4, 1), ("B", 7, 1)],
    [],
]
ALONG = {0: (3, 2, 1), 3: (6, 5, 4)}


def kernel(q_ref, k_ref, v_ref, lens_ref, order_ref, out_ref,
           buf, ext, qx, qtmp, vtmp, acc, top, send_sem, recv_sem, core_sem, local_sem):
    head = lax.axis_index("head")
    ctx = lax.axis_index("ctx")
    core = lax.rem(head, 2)
    y_lo = lax.rem(head // 2, 2)
    x_lo = ctx // RING
    z = lax.rem(ctx, RING)
    group = head // 4
    own = 2 * ctx
    other_x = 1 - x_lo

    local = [
        pltpu.make_async_copy(v_ref.at[group], vtmp, local_sem.at[0]),
        pltpu.make_async_copy(k_ref.at[group, y_lo], buf.at[0, 64], local_sem.at[1]),
        pltpu.make_async_copy(k_ref.at[group, 1 - y_lo], buf.at[0, 65], local_sem.at[2]),
        pltpu.make_async_copy(q_ref, qtmp, local_sem.at[3]),
    ]
    for copy in local:
        copy.start()

    empty_places = (PLACE[None, 0], PLACE[None, 1])
    for p in empty_places:
        buf[0, p] = jnp.zeros((SPAN, DH), jnp.bfloat16)
        buf[1, p] = jnp.zeros((SPAN, DH), jnp.bfloat16)

    def along(distance):
        return {"ctx": x_lo * RING + lax.rem(z + distance + RING, RING)}

    to_x = {"ctx": other_x * RING + z}
    to_y = {"head": head + 2 - 4 * y_lo}
    to_core = {"head": head + 1 - 2 * core}

    if COMM:
        barrier = pltpu.get_barrier_semaphore()
        for device in [along(d) for d in (1, -1, 2, -2, 3, -3)] + [to_x, to_y, to_core]:
            pl.semaphore_signal(barrier, inc=1, device_id=device, device_id_type=MESH)

    def unit(source, target, device):
        return pltpu.make_async_remote_copy(
            src_ref=buf.at[core, source],
            dst_ref=buf.at[core, target],
            send_sem=send_sem,
            recv_sem=recv_sem.at[target],
            device_id=device,
            device_id_type=MESH,
        )

    def pair(kv, n):
        return pltpu.make_async_remote_copy(
            src_ref=buf.at[kv, pl.ds(4 * n, 4)],
            dst_ref=buf.at[kv, pl.ds(4 * n, 4)],
            send_sem=send_sem,
            recv_sem=core_sem.at[n],
            device_id=to_core,
            device_id_type=MESH,
        )

    def send(source, target, device):
        if COMM:
            unit(source, target, device).start()

    def ways(distance):
        return (1,) if distance in (0, 8) else (1, -1)

    missing = [sum(slot is not None for slot in p) * 2 for p in PAIRS]

    def relay(kind, distance, side):
        signed = [-way * distance if distance not in (0, 8) else distance for way in ways(distance)]
        here = [PLACE[(kind, r), side] for r in signed]
        for p in here:
            if COMM:
                unit(p, p, to_core).wait_recv()
        if kind == "A":
            if distance == 6 and side == 0:
                up, down = PLACE[("A", -6), 0], PLACE[("A", 6), 0]
                send(up + core * (down - up), PLACE[("A", 8), 0], along(2 - 4 * core))
                for way in (1, -1):
                    send(PLACE[("A", -6 * way), 0], PLACE[("A", -7 * way), 0], along(way))
            if side == 0:
                for far in ALONG.get(distance, ()):
                    for way in (1, -1):
                        send(PLACE[("A", -way * distance), 0], PLACE[("A", -way * far), 0],
                             along(way * (far - distance)))
                if distance != 1:
                    for r, p in zip(signed, here):
                        send(p, PLACE[("A", r), 1], to_y)
            if side == 0 or distance in OVER_X:
                for r, p in zip(signed, here):
                    send(p, PLACE[("B", r), side], to_x)
        elif side == 0 and distance and distance not in OVER_X:
            for r, p in zip(signed, here):
                send(p, PLACE[("B", r), 1], to_y)
        for r in signed:
            n = [k for k, p in enumerate(PAIRS) if (kind, r) in p][0]
            missing[n] -= 1
            if missing[n] == 0 and COMM:
                pair(core, n).start()

    def attend(keys, values, own_slot=False):
        if not COMPUTE:
            return
        values = jnp.concatenate(
            [values, jnp.ones((ONES, values.shape[1]), jnp.bfloat16)], axis=0
        )
        scores = jnp.dot(keys, qx[...], preferred_element_type=jnp.float32)
        if own_slot:
            key_row = lax.broadcasted_iota(jnp.int32, scores.shape, 0)
            query_row = lax.broadcasted_iota(jnp.int32, scores.shape, 1) % (2 * SPAN)
            later = (key_row > query_row) & ((key_row >= SPAN) == (query_row >= SPAN))
            scores = jnp.where(later, -BIG, scores)
        scores = scores * FACTOR
        highest = jnp.max(scores, axis=0, keepdims=True)
        if own_slot:
            new_top = highest
        else:
            old_top = top[0:1, :]
            new_top = jnp.maximum(old_top, highest)
        weights = jnp.exp2(scores - new_top).astype(jnp.bfloat16)
        mixed = jnp.dot(values, weights, preferred_element_type=jnp.float32)
        if own_slot:
            acc[...] = mixed
        else:
            acc[...] = acc[...] * jnp.exp2(old_top - new_top) + mixed
        top[0:1, :] = new_top

    local[0].wait()
    for j in (0, 1):
        block = vtmp[j].astype(jnp.float32)
        buf[1, 64 + (y_lo if j == 0 else 1 - y_lo)] = block.T.astype(jnp.bfloat16)
    local[1].wait()
    local[2].wait()
    if COMM:
        pl.semaphore_wait(barrier, 9)
    for distance in ALONG[0]:
        for way in (1, -1):
            send(64, PLACE[("A", -way * distance), 0], along(way * distance))
    for side in (0, 1):
        send(64 + side, PLACE[("B", 0), side], to_x)
    for way in (1, -1):
        send(65, PLACE[("A", -way), 1], along(way))

    def borders(lane):
        opens = jnp.where(lane < SPANS, lane * SPAN, 1 << 20)
        closes = jnp.where(lane < SPANS, lane * SPAN + SPAN, 1 << 20)
        end = jnp.int32(0)
        for d in range(DOCS):
            opens = jnp.where(lane == SPANS + d, end, opens)
            end = end + lens_ref[d]
            closes = jnp.where(lane == SPANS + d, end if d < DOCS - 1 else 1 << 20, closes)
        return opens, closes

    lane = lax.broadcasted_iota(jnp.int32, (1, DH), 1)
    opens, closes = borders(lane)
    row = lax.broadcasted_iota(jnp.int32, (DH, 1), 0)
    row_opens, row_closes = borders(row)
    in_span = lax.broadcasted_iota(jnp.int32, (SPAN, 1), 0)

    for (slot, side), p in PLACE.items():
        if slot is None:
            marks = jnp.where(lane == SPANS + DOCS, 1.0, 0.0) + jnp.zeros((SPAN, 1), jnp.float32)
        else:
            kind, r = slot
            first = 2 * ((x_lo if kind == "A" else other_x) * RING + lax.rem(z + r + RING, RING))
            position = order_ref[first + (y_lo if side == 0 else 1 - y_lo)] * SPAN + in_span
            marks = jnp.where((position >= opens) & (position < closes), 1.0, 0.0)
        ext[p] = marks.astype(jnp.bfloat16)

    for j in (0, 1):
        position = order_ref[own + j] * SPAN + lax.broadcasted_iota(jnp.int32, (1, SPAN), 1)
        outside = jnp.where((position >= row_opens) & (position < row_closes), 0.0, -BIG)
        after = jnp.where(row > order_ref[own + j], -BIG, 0.0) + jnp.zeros((1, SPAN), jnp.float32)
        last = jnp.where(row == SPANS + DOCS, -BIG, 0.0) + jnp.zeros((1, SPAN), jnp.float32)
        side_q = jnp.where(row < SPANS, after, jnp.where(row < SPANS + DOCS, outside, last))
        for h in range(4):
            qx[DH:, (2 * h + j) * SPAN:(2 * h + j + 1) * SPAN] = side_q.astype(jnp.bfloat16)
    local[3].wait()
    for h in range(4):
        qx[:DH, 2 * h * SPAN:2 * (h + 1) * SPAN] = (
            qtmp[h].astype(jnp.float32).T.astype(jnp.bfloat16)
        )

    natural = [64 + y_lo, 65 - y_lo]
    attend(
        jnp.concatenate([jnp.concatenate([buf[0, p], ext[p]], axis=1) for p in natural], axis=0),
        jnp.concatenate([buf[1, p] for p in natural], axis=1),
        own_slot=True,
    )

    def turn(i, carry):
        for k, events in enumerate(ORDER):
            if events:
                @pl.when(i == k)
                def _():
                    for kind, distance, side in events:
                        relay(kind, distance, side)

        if COMM:
            pair(1 - core, 2 * i).wait_recv()
            pair(1 - core, 2 * i + 1).wait_recv()
        eight = pl.ds(8 * i, 8)
        attend(
            jnp.concatenate(
                [buf[0, eight].reshape(8 * SPAN, DH), ext[eight].reshape(8 * SPAN, DH)], axis=1
            ),
            jnp.concatenate([buf[1, 8 * i + j] for j in range(8)], axis=1),
        )
        return carry

    lax.fori_loop(0, len(ORDER), turn, 0)

    if COMPUTE:
        result = acc[:DH, :] / acc[DH:DH + 1, :]
        for h in range(4):
            out_ref[h] = result[:, 2 * h * SPAN:2 * (h + 1) * SPAN].T.astype(jnp.bfloat16)
    else:
        for h in range(4):
            out_ref[h] = (buf[0, 2 * h].astype(jnp.float32) + buf[1, 2 * h + 9]).astype(jnp.bfloat16)[:1, :] + jnp.zeros((256, DH), jnp.bfloat16)
    if COMM:
        pltpu.make_async_copy(buf.at[:, pl.ds(0, 63)], buf.at[:, pl.ds(0, 63)], send_sem).wait()


def body(queries, key_heads, value_heads, doc_lengths, span_order):
    heads, rows, _ = queries.shape
    shape = (key_heads.shape[0], 2, SPAN, DH)
    return pl.pallas_call(
        kernel,
        out_shape=jax.ShapeDtypeStruct(queries.shape, jnp.bfloat16),
        in_specs=[
            pl.BlockSpec(memory_space=pl.ANY),
            pl.BlockSpec(memory_space=pl.ANY),
            pl.BlockSpec(memory_space=pl.ANY),
            pl.BlockSpec(memory_space=pltpu.SMEM),
            pl.BlockSpec(memory_space=pltpu.SMEM),
        ],
        out_specs=pl.BlockSpec(memory_space=pltpu.VMEM),
        scratch_shapes=[
            pltpu.VMEM((2, SPANS + 2, SPAN, DH), jnp.bfloat16),
            pltpu.VMEM((SPANS + 2, SPAN, DH), jnp.bfloat16),
            pltpu.VMEM((2 * DH, heads * rows), jnp.bfloat16),
            pltpu.VMEM((heads, rows, DH), jnp.bfloat16),
            pltpu.VMEM((2, SPAN, DH), jnp.bfloat16),
            pltpu.VMEM((DH + ONES, heads * rows), jnp.float32),
            pltpu.VMEM((8, heads * rows), jnp.float32),
            pltpu.SemaphoreType.DMA,
            pltpu.SemaphoreType.DMA((SPANS,)),
            pltpu.SemaphoreType.DMA((len(PAIRS),)),
            pltpu.SemaphoreType.DMA((4,)),
        ],
        compiler_params=pltpu.CompilerParams(
            collective_id=0 if COMM else None, has_side_effects=True, vmem_limit_bytes=62 * 2**20
        ),
        cost_estimate=pl.CostEstimate(
            flops=4 * heads * rows * SPANS * SPAN * DH,
            bytes_accessed=2**20,
            transcendentals=heads * rows * SPANS * SPAN,
        ),
    )(queries, key_heads.reshape(shape), value_heads.reshape(shape), doc_lengths, span_order)


def solution(mesh):
    return jax.shard_map(
        body,
        mesh=mesh,
        in_specs=(P("head", "ctx", None), P(None, "ctx", None), P(None, "ctx", None), P(), P()),
        out_specs=P("head", "ctx", None),
        check_vma=False,
    )
```

time: 51.5 us -> 47.6 us (0.924)
  Pallas kernels: 49.6 us -> 45.7 us
    pallas_call x1, Pallas kernels: 49.6 us -> 45.7 us  [body(): pl.pallas_call(kernel, out_shape=jax.ShapeDtypeStruct(queries.shape, jnp....]
where the time goes in v3:
time: 47.6 us; the launch traced here: 47.4 us
  Pallas kernels  45.7 us (96%)
  local copies, waits for them, and re-layouts  1.67 us (4%)
    pallas_call x1, Pallas kernels, body(): pl.pallas_call(kernel, out_shape=jax.ShapeDtypeStruct(queries.shape, jnp....  45.7 us
    unnamed x1, local copies, waits for them, and re-layouts  1.67 us

profile of v3, /device:TPU:1, one launch (start us, length us, event | category | flops | bytes accessed | tf_op | source)
XLA Modules:
  0.0 47.4 jit_solution(18395843110139004195)
XLA Ops:
  0.0 45.7 %shard_map.55 = bf16[4,256,128]{2,1,0:T(8,128)(2,1)} custom-call(bf16[4,256,128]{2,1,0:T(8,128)(2,1)} %q_ref.1, bf16[4,2,128,128]{3,2,1,0:T(8,128)(2,1)} %bitcast.2, bf16[4,2,128,128]{3,2,1,0:T(8,128)(2,1)} %bitcast.3, s32[16]{0:T(128)} %lens_ref.1, s32[64]{0:T(128)} %order_ref.1), custom_call_target="tpu_custom_call" | custom-call | flops 4294967296 | bytes 1048576 | tf_op jit(solution)/shard_map/pallas_call | solution.py:281
  45.7 1.7 %copy.7 = bf16[4,256,128]{2,1,0:T(8,128)(2,1)} copy(bf16[4,256,128]{2,1,0:T(8,128)(2,1)} %shard_map.55) | data formatting | bytes 524288

commit v4 on v3

--- a/solution.py
+++ b/solution.py
@@ -16,45 +16,57 @@
 BIG = 131072.0
 FACTOR = math.log2(math.e) / math.sqrt(DH)
 ONES = 16
-COMM = True
-COMPUTE = True
-
-
-PAIRS = [
-    (("A", 1), ("A", -1)), (("A", 3), ("A", -3)),
-    (("A", 2), ("A", -2)), (("B", 1), ("B", -1)),
-    (("B", 3), ("B", -3)), (("A", 6), ("A", -6)),
-    (("B", 2), ("B", -2)), (("A", 5), ("A", -5)),
-    (("A", 4), ("A", -4)), (("A", 8), ("B", 0)),
-    (("B", 6), ("B", -6)), (("A", 7), ("A", -7)),
-    (("B", 5), ("B", -5)), (("B", 8), None),
-    (("B", 4), ("B", -4)), (("B", 7), ("B", -7)),
+
+
+BLOCKS = [
+    [("B", 0, 0), ("B", 0, 1), ("A", 3, 0), ("A", 2, 0), ("A", 1, 0)],
+    [("A", 1, 1), ("A", 3, 1), ("B", 3, 0), ("A", 6, 0)],
+    [("A", 2, 1), ("B", 2, 0), ("A", 5, 0), ("A", 4, 0)],
+    [("B", 1, 0), ("B", 1, 1), ("B", 3, 1), ("A", 8, 0), None],
+    [("A", 7, 0), ("B", 6, 0), ("A", 6, 1), ("B", 5, 0)],
+    [("B", 2, 1), ("B", 4, 0), ("A", 5, 1), ("B", 8, 0), None],
+    [("A", 4, 1), ("B", 7, 0), ("A", 8, 1), ("B", 6, 1), ("B", 8, 1)],
+    [("A", 7, 1), ("B", 5, 1), ("B", 4, 1), ("B", 7, 1)],
 ]
-PLACE = {}
-for _n, _pair in enumerate(PAIRS):
-    for _m, _slot in enumerate(_pair):
-        for _side in (0, 1):
-            PLACE[_slot, _side] = 4 * _n + 2 * _side + _m
-PLACE[("A", 0), 0] = 64
-PLACE[("A", 0), 1] = 65
-OVER_X = (1, 4, 5, 6)
 ORDER = [
     [("B", 0, 0), ("B", 0, 1), ("A", 3, 0), ("A", 2, 0), ("A", 1, 0), ("A", 1, 1),
-     ("A", 3, 1), ("B", 3, 0), ("A", 6, 0)],
-    [("A", 2, 1), ("B", 2, 0), ("A", 5, 0), ("A", 4, 0), ("B", 1, 0), ("B", 1, 1),
-     ("B", 3, 1), ("A", 8, 0), ("A", 7, 0)],
-    [("B", 6, 0), ("A", 6, 1), ("B", 5, 0)],
-    [("B", 2, 1), ("B", 4, 0), ("A", 5, 1), ("B", 8, 0)],
-    [("A", 4, 1), ("B", 7, 0), ("A", 8, 1)],
-    [("B", 6, 1), ("A", 7, 1), ("B", 8, 1), ("B", 5, 1)],
-    [("B", 4, 1), ("B", 7, 1)],
+     ("A", 3, 1), ("B", 3, 0), ("A", 6, 0), ("A", 2, 1), ("B", 2, 0), ("A", 5, 0), ("A", 4, 0),
+     ("B", 1, 0)],
+    [("B", 1, 1), ("B", 3, 1), ("A", 8, 0), ("A", 7, 0)],
+    [("B", 6, 0), ("A", 6, 1)],
+    [("B", 5, 0), ("B", 2, 1), ("B", 4, 0), ("A", 5, 1), ("B", 8, 0)],
+    [("A", 4, 1), ("B", 7, 0)],
+    [("A", 8, 1), ("B", 6, 1), ("A", 7, 1), ("B", 8, 1)],
+    [("B", 5, 1), ("B", 4, 1), ("B", 7, 1)],
     [],
 ]
+
+
+def signed(distance):
+    return (distance,) if distance in (0, 8) else (-distance, distance)
+
+
+SPOTS = []
+for _block in BLOCKS:
+    for _batch in _block:
+        if _batch is None:
+            SPOTS.append(None)
+        else:
+            SPOTS.extend(((_batch[0], r), _batch[2]) for r in signed(_batch[1]))
+SPOTS += [(("A", 0), 0), (("A", 0), 1)]
+PLACE = {spot: p for p, spot in enumerate(SPOTS) if spot is not None}
+EMPTY = [p for p, spot in enumerate(SPOTS) if spot is None]
+LAST = [
+    [e for events in ORDER for e in events
+     if any(((e[0], r), e[2]) in SPOTS[n:n + 4] for r in signed(e[1]))][-1]
+    for n in range(0, SPANS, 4)
+]
+OVER_X = (1, 4, 5, 6)
 ALONG = {0: (3, 2, 1), 3: (6, 5, 4)}
 
 
-def kernel(q_ref, k_ref, v_ref, lens_ref, order_ref, out_ref,
-           buf, ext, qx, qtmp, vtmp, acc, top, send_sem, recv_sem, core_sem, local_sem):
+def kernel(q_ref, k_ref, v_ref, lens_in, order_in, out_ref,
+           lens_ref, order_ref, buf, ext, qx, qtmp, vtmp, acc, top, send_sem, recv_sem, core_sem, local_sem):
     head = lax.axis_index("head")
     ctx = lax.axis_index("ctx")
     core = lax.rem(head, 2)
@@ -69,13 +81,14 @@
         pltpu.make_async_copy(v_ref.at[group], vtmp, local_sem.at[0]),
         pltpu.make_async_copy(k_ref.at[group, y_lo], buf.at[0, 64], local_sem.at[1]),
         pltpu.make_async_copy(k_ref.at[group, 1 - y_lo], buf.at[0, 65], local_sem.at[2]),
+        pltpu.make_async_copy(lens_in, lens_ref, local_sem.at[4]),
+        pltpu.make_async_copy(order_in, order_ref, local_sem.at[5]),
         pltpu.make_async_copy(q_ref, qtmp, local_sem.at[3]),
     ]
     for copy in local:
         copy.start()
 
-    empty_places = (PLACE[None, 0], PLACE[None, 1])
-    for p in empty_places:
+    for p in EMPTY:
         buf[0, p] = jnp.zeros((SPAN, DH), jnp.bfloat16)
         buf[1, p] = jnp.zeros((SPAN, DH), jnp.bfloat16)
 
@@ -86,10 +99,9 @@
     to_y = {"head": head + 2 - 4 * y_lo}
     to_core = {"head": head + 1 - 2 * core}
 
-    if COMM:
-        barrier = pltpu.get_barrier_semaphore()
-        for device in [along(d) for d in (1, -1, 2, -2, 3, -3)] + [to_x, to_y, to_core]:
-            pl.semaphore_signal(barrier, inc=1, device_id=device, device_id_type=MESH)
+    barrier = pltpu.get_barrier_semaphore()
+    for device in [along(d) for d in (1, -1, 2, -2, 3, -3)] + [to_x, to_y, to_core]:
+        pl.semaphore_signal(barrier, inc=1, device_id=device, device_id_type=MESH)
 
     def unit(source, target, device):
         return pltpu.make_async_remote_copy(
@@ -112,20 +124,13 @@
         )
 
     def send(source, target, device):
-        if COMM:
-            unit(source, target, device).start()
-
-    def ways(distance):
-        return (1,) if distance in (0, 8) else (1, -1)
-
-    missing = [sum(slot is not None for slot in p) * 2 for p in PAIRS]
+        unit(source, target, device).start()
 
     def relay(kind, distance, side):
-        signed = [-way * distance if distance not in (0, 8) else distance for way in ways(distance)]
-        here = [PLACE[(kind, r), side] for r in signed]
+        rels = signed(distance)
+        here = [PLACE[(kind, r), side] for r in rels]
         for p in here:
-            if COMM:
-                unit(p, p, to_core).wait_recv()
+            unit(p, p, to_core).wait_recv()
         if kind == "A":
             if distance == 6 and side == 0:
                 up, down = PLACE[("A", -6), 0], PLACE[("A", 6), 0]
@@ -138,23 +143,19 @@
                         send(PLACE[("A", -way * distance), 0], PLACE[("A", -way * far), 0],
                              along(way * (far - distance)))
                 if distance != 1:
-                    for r, p in zip(signed, here):
+                    for r, p in zip(rels, here):
                         send(p, PLACE[("A", r), 1], to_y)
             if side == 0 or distance in OVER_X:
-                for r, p in zip(signed, here):
+                for r, p in zip(rels, here):
                     send(p, PLACE[("B", r), side], to_x)
         elif side == 0 and distance and distance not in OVER_X:
-            for r, p in zip(signed, here):
+            for r, p in zip(rels, here):
                 send(p, PLACE[("B", r), 1], to_y)
-        for r in signed:
-            n = [k for k, p in enumerate(PAIRS) if (kind, r) in p][0]
-            missing[n] -= 1
-            if missing[n] == 0 and COMM:
+        for n, event in enumerate(LAST):
+            if event == (kind, distance, side):
                 pair(core, n).start()
 
     def attend(keys, values, own_slot=False):
-        if not COMPUTE:
-            return
         values = jnp.concatenate(
             [values, jnp.ones((ONES, values.shape[1]), jnp.bfloat16)], axis=0
         )
@@ -185,8 +186,7 @@
         buf[1, 64 + (y_lo if j == 0 else 1 - y_lo)] = block.T.astype(jnp.bfloat16)
     local[1].wait()
     local[2].wait()
-    if COMM:
-        pl.semaphore_wait(barrier, 9)
+    pl.semaphore_wait(barrier, 9)
     for distance in ALONG[0]:
         for way in (1, -1):
             send(64, PLACE[("A", -way * distance), 0], along(way * distance))
@@ -194,6 +194,9 @@
         send(64 + side, PLACE[("B", 0), side], to_x)
     for way in (1, -1):
         send(65, PLACE[("A", -way), 1], along(way))
+
+    local[3].wait()
+    local[4].wait()
 
     def borders(lane):
         opens = jnp.where(lane < SPANS, lane * SPAN, 1 << 20)
@@ -211,11 +214,11 @@
     row_opens, row_closes = borders(row)
     in_span = lax.broadcasted_iota(jnp.int32, (SPAN, 1), 0)
 
-    for (slot, side), p in PLACE.items():
-        if slot is None:
+    for p, spot in enumerate(SPOTS):
+        if spot is None:
             marks = jnp.where(lane == SPANS + DOCS, 1.0, 0.0) + jnp.zeros((SPAN, 1), jnp.float32)
         else:
-            kind, r = slot
+            (kind, r), side = spot
             first = 2 * ((x_lo if kind == "A" else other_x) * RING + lax.rem(z + r + RING, RING))
             position = order_ref[first + (y_lo if side == 0 else 1 - y_lo)] * SPAN + in_span
             marks = jnp.where((position >= opens) & (position < closes), 1.0, 0.0)
@@ -229,7 +232,7 @@
         side_q = jnp.where(row < SPANS, after, jnp.where(row < SPANS + DOCS, outside, last))
         for h in range(4):
             qx[DH:, (2 * h + j) * SPAN:(2 * h + j + 1) * SPAN] = side_q.astype(jnp.bfloat16)
-    local[3].wait()
+    local[5].wait()
     for h in range(4):
         qx[:DH, 2 * h * SPAN:2 * (h + 1) * SPAN] = (
             qtmp[h].astype(jnp.float32).T.astype(jnp.bfloat16)
@@ -250,9 +253,8 @@
                     for kind, distance, side in events:
                         relay(kind, distance, side)
 
-        if COMM:
-            pair(1 - core, 2 * i).wait_recv()
-            pair(1 - core, 2 * i + 1).wait_recv()
+        pair(1 - core, 2 * i).wait_recv()
+        pair(1 - core, 2 * i + 1).wait_recv()
         eight = pl.ds(8 * i, 8)
         attend(
             jnp.concatenate(
@@ -264,15 +266,10 @@
 
     lax.fori_loop(0, len(ORDER), turn, 0)
 
-    if COMPUTE:
-        result = acc[:DH, :] / acc[DH:DH + 1, :]
-        for h in range(4):
-            out_ref[h] = result[:, 2 * h * SPAN:2 * (h + 1) * SPAN].T.astype(jnp.bfloat16)
-    else:
-        for h in range(4):
-            out_ref[h] = (buf[0, 2 * h].astype(jnp.float32) + buf[1, 2 * h + 9]).astype(jnp.bfloat16)[:1, :] + jnp.zeros((256, DH), jnp.bfloat16)
-    if COMM:
-        pltpu.make_async_copy(buf.at[:, pl.ds(0, 63)], buf.at[:, pl.ds(0, 63)], send_sem).wait()
+    result = acc[:DH, :] / acc[DH:DH + 1, :]
+    for h in range(4):
+        out_ref[h] = result[:, 2 * h * SPAN:2 * (h + 1) * SPAN].T.astype(jnp.bfloat16)
+    pltpu.make_async_copy(buf.at[:, pl.ds(0, 63)], buf.at[:, pl.ds(0, 63)], send_sem).wait()
 
 
 def body(queries, key_heads, value_heads, doc_lengths, span_order):
@@ -285,11 +282,13 @@
             pl.BlockSpec(memory_space=pl.ANY),
             pl.BlockSpec(memory_space=pl.ANY),
             pl.BlockSpec(memory_space=pl.ANY),
-            pl.BlockSpec(memory_space=pltpu.SMEM),
-            pl.BlockSpec(memory_space=pltpu.SMEM),
+            pl.BlockSpec(memory_space=pl.ANY),
+            pl.BlockSpec(memory_space=pl.ANY),
         ],
         out_specs=pl.BlockSpec(memory_space=pltpu.VMEM),
         scratch_shapes=[
+            pltpu.SMEM((DOCS,), jnp.int32),
+            pltpu.SMEM((SPANS,), jnp.int32),
             pltpu.VMEM((2, SPANS + 2, SPAN, DH), jnp.bfloat16),
             pltpu.VMEM((SPANS + 2, SPAN, DH), jnp.bfloat16),
             pltpu.VMEM((2 * DH, heads * rows), jnp.bfloat16),
@@ -299,11 +298,11 @@
             pltpu.VMEM((8, heads * rows), jnp.float32),
             pltpu.SemaphoreType.DMA,
             pltpu.SemaphoreType.DMA((SPANS,)),
-            pltpu.SemaphoreType.DMA((len(PAIRS),)),
-            pltpu.SemaphoreType.DMA((4,)),
+            pltpu.SemaphoreType.DMA((SPANS // 4,)),
+            pltpu.SemaphoreType.DMA((6,)),
         ],
         compiler_params=pltpu.CompilerParams(
-            collective_id=0 if COMM else None, has_side_effects=True, vmem_limit_bytes=62 * 2**20
+            collective_id=0, has_side_effects=True, vmem_limit_bytes=62 * 2**20
         ),
         cost_estimate=pl.CostEstimate(
             flops=4 * heads * rows * SPANS * SPAN * DH,

time: 47.6 us -> 42.5 us (0.89)
  Pallas kernels: 45.7 us -> 40.7 us
    pallas_call x1, Pallas kernels: 45.7 us -> 40.7 us  [body(): pl.pallas_call(kernel, out_shape=jax.ShapeDtypeStruct(queries.shape, jnp....]
where the time goes in v4:
time: 42.5 us; the launch traced here: 42.4 us
  Pallas kernels  40.7 us (96%)
  local copies, waits for them, and re-layouts  1.67 us (4%)
    pallas_call x1, Pallas kernels, body(): pl.pallas_call(kernel, out_shape=jax.ShapeDtypeStruct(queries.shape, jnp....  40.7 us
    unnamed x1, local copies, waits for them, and re-layouts  1.67 us

profile of v4, /device:TPU:1, one launch (start us, length us, event | category | flops | bytes accessed | tf_op | source)
XLA Modules:
  0.0 42.4 jit_solution(3884191472521889116)
XLA Ops:
  0.0 40.7 %shard_map.55 = bf16[4,256,128]{2,1,0:T(8,128)(2,1)} custom-call(bf16[4,256,128]{2,1,0:T(8,128)(2,1)} %q_ref.1, bf16[4,2,128,128]{3,2,1,0:T(8,128)(2,1)} %bitcast.2, bf16[4,2,128,128]{3,2,1,0:T(8,128)(2,1)} %bitcast.3, s32[16]{0:T(128)} %lens_in.1, s32[64]{0:T(128)} %order_in.1), custom_call_target="tpu_custom_call" | custom-call | flops 4294967296 | bytes 1048576 | tf_op jit(solution)/shard_map/pallas_call | solution.py:278
  40.7 1.7 %copy.7 = bf16[4,256,128]{2,1,0:T(8,128)(2,1)} copy(bf16[4,256,128]{2,1,0:T(8,128)(2,1)} %shard_map.55) | data formatting | bytes 524288

commit v5 on v4

--- a/solution.py
+++ b/solution.py
@@ -302,7 +302,7 @@
             pltpu.SemaphoreType.DMA((6,)),
         ],
         compiler_params=pltpu.CompilerParams(
-            collective_id=0, has_side_effects=True, vmem_limit_bytes=62 * 2**20
+            collective_id=0, has_side_effects=True, vmem_limit_bytes=54784 * 2**10
         ),
         cost_estimate=pl.CostEstimate(
             flops=4 * heads * rows * SPANS * SPAN * DH,

time: 42.5 us -> 41.5 us (0.976)
  Pallas kernels: 40.7 us -> 40 us
    pallas_call x1, Pallas kernels: 40.7 us -> 40 us  [body(): pl.pallas_call(kernel, out_shape=jax.ShapeDtypeStruct(queries.shape, jnp....]
    unnamed x1 -> x5, local copies, waits for them, and re-layouts: 1.67 us -> 1.37 us
where the time goes in v5:
time: 41.5 us; the launch traced here: 41.4 us
  Pallas kernels  40 us (96%)
  local copies, waits for them, and re-layouts  1.37 us (3%)
    pallas_call x1, Pallas kernels, body(): pl.pallas_call(kernel, out_shape=jax.ShapeDtypeStruct(queries.shape, jnp....  40 us
    unnamed x5, local copies, waits for them, and re-layouts  1.37 us

profile of v5, /device:TPU:1, one launch (start us, length us, event | category | flops | bytes accessed | tf_op | source)
XLA Modules:
  0.0 41.4 jit_solution(9420275229733301676)
XLA Ops:
  0.0 0.0 copy-start
  0.0 0.0 copy-start.1
  0.0 0.7 %copy-done = s32[16]{0:T(128)S(1)} copy-done((s32[16]{0:T(128)S(1)}, s32[16]{0:T(128)}, u32[]{:S(2)}) %copy-start) | copy-done | bytes 88
  0.7 0.0 copy-done.1
  0.7 40.0 %shard_map.55 = bf16[4,256,128]{2,1,0:T(8,128)(2,1)S(1)} custom-call(bf16[4,256,128]{2,1,0:T(8,128)(2,1)} %q_ref.1, bf16[4,2,128,128]{3,2,1,0:T(8,128)(2,1)} %bitcast.2, bf16[4,2,128,128]{3,2,1,0:T(8,128)(2,1)} %bitcast.3, s32[16]{0:T(128)S(1)} %copy-done, s32[64]{0:T(128)S(1)} %copy-done.1), custom_call_target="tpu_custom_call" | custom-call | flops 4294967296 | bytes 1048576 | tf_op jit(solution)/shard_map/pallas_call | solution.py:278
  40.7 0.7 %copy.7 = bf16[4,256,128]{2,1,0:T(8,128)(2,1)} copy(bf16[4,256,128]{2,1,0:T(8,128)(2,1)S(1)} %shard_map.55) | data formatting | bytes 524288
Async XLA Ops:
  0.0 0.7 %copy-start = (s32[16]{0:T(128)S(1)}, s32[16]{0:T(128)}, u32[]{:S(2)}) copy-start(s32[16]{0:T(128)} %lens_in.1) | copy-start | bytes 196
  0.0 0.7 %copy-start.1 = (s32[64]{0:T(128)S(1)}, s32[64]{0:T(128)}, u32[]{:S(2)}) copy-start(s32[64]{0:T(128)} %order_in.1) | copy-start | bytes 772

commit v6 on v5

--- a/solution.py
+++ b/solution.py
@@ -30,9 +30,8 @@
 ]
 ORDER = [
     [("B", 0, 0), ("B", 0, 1), ("A", 3, 0), ("A", 2, 0), ("A", 1, 0), ("A", 1, 1),
-     ("A", 3, 1), ("B", 3, 0), ("A", 6, 0), ("A", 2, 1), ("B", 2, 0), ("A", 5, 0), ("A", 4, 0),
-     ("B", 1, 0)],
-    [("B", 1, 1), ("B", 3, 1), ("A", 8, 0), ("A", 7, 0)],
+     ("A", 3, 1), ("B", 3, 0), ("A", 6, 0), ("A", 2, 1), ("B", 2, 0), ("A", 5, 0)],
+    [("A", 4, 0), ("B", 1, 0), ("B", 1, 1), ("B", 3, 1), ("A", 8, 0), ("A", 7, 0)],
     [("B", 6, 0), ("A", 6, 1)],
     [("B", 5, 0), ("B", 2, 1), ("B", 4, 0), ("A", 5, 1), ("B", 8, 0)],
     [("A", 4, 1), ("B", 7, 0)],
@@ -142,12 +141,12 @@
                     for way in (1, -1):
                         send(PLACE[("A", -way * distance), 0], PLACE[("A", -way * far), 0],
                              along(way * (far - distance)))
-                if distance != 1:
-                    for r, p in zip(rels, here):
-                        send(p, PLACE[("A", r), 1], to_y)
             if side == 0 or distance in OVER_X:
                 for r, p in zip(rels, here):
                     send(p, PLACE[("B", r), side], to_x)
+            if side == 0 and distance != 1:
+                for r, p in zip(rels, here):
+                    send(p, PLACE[("A", r), 1], to_y)
         elif side == 0 and distance and distance not in OVER_X:
             for r, p in zip(rels, here):
                 send(p, PLACE[("B", r), 1], to_y)

time: 41.5 us -> 41.5 us (level)
  no operation moved by 1% of the time
where the time goes in v6:
time: 41.5 us; the launch traced here: 41.3 us
  Pallas kernels  40 us (96%)
  local copies, waits for them, and re-layouts  1.37 us (3%)
    pallas_call x1, Pallas kernels, body(): pl.pallas_call(kernel, out_shape=jax.ShapeDtypeStruct(queries.shape, jnp....  40 us
    unnamed x5, local copies, waits for them, and re-layouts  1.37 us

profile of v6, /device:TPU:1, one launch (start us, length us, event | category | flops | bytes accessed | tf_op | source)
XLA Modules:
  0.0 41.3 jit_solution(9387652943682167819)
XLA Ops:
  0.0 0.0 copy-start
  0.0 0.0 copy-start.1
  0.0 0.7 %copy-done = s32[16]{0:T(128)S(1)} copy-done((s32[16]{0:T(128)S(1)}, s32[16]{0:T(128)}, u32[]{:S(2)}) %copy-start) | copy-done | bytes 88
  0.7 0.0 copy-done.1
  0.7 40.0 %shard_map.55 = bf16[4,256,128]{2,1,0:T(8,128)(2,1)S(1)} custom-call(bf16[4,256,128]{2,1,0:T(8,128)(2,1)} %q_ref.1, bf16[4,2,128,128]{3,2,1,0:T(8,128)(2,1)} %bitcast.2, bf16[4,2,128,128]{3,2,1,0:T(8,128)(2,1)} %bitcast.3, s32[16]{0:T(128)S(1)} %copy-done, s32[64]{0:T(128)S(1)} %copy-done.1), custom_call_target="tpu_custom_call" | custom-call | flops 4294967296 | bytes 1048576 | tf_op jit(solution)/shard_map/pallas_call | solution.py:277
  40.6 0.7 %copy.7 = bf16[4,256,128]{2,1,0:T(8,128)(2,1)} copy(bf16[4,256,128]{2,1,0:T(8,128)(2,1)S(1)} %shard_map.55) | data formatting | bytes 524288
Async XLA Ops:
  0.0 0.7 %copy-start = (s32[16]{0:T(128)S(1)}, s32[16]{0:T(128)}, u32[]{:S(2)}) copy-start(s32[16]{0:T(128)} %lens_in.1) | copy-start | bytes 196
  0.0 0.7 %copy-start.1 = (s32[64]{0:T(128)S(1)}, s32[64]{0:T(128)}, u32[]{:S(2)}) copy-start(s32[64]{0:T(128)} %order_in.1) | copy-start | bytes 772

commit v7 on v6

--- a/solution.py
+++ b/solution.py
@@ -179,21 +179,23 @@
             acc[...] = acc[...] * jnp.exp2(old_top - new_top) + mixed
         top[0:1, :] = new_top
 
+    def turned(side):
+        block = vtmp[y_lo if side == 0 else 1 - y_lo].astype(jnp.float32)
+        buf[1, 64 + side] = block.T.astype(jnp.bfloat16)
+
     local[0].wait()
-    for j in (0, 1):
-        block = vtmp[j].astype(jnp.float32)
-        buf[1, 64 + (y_lo if j == 0 else 1 - y_lo)] = block.T.astype(jnp.bfloat16)
+    turned(0)
     local[1].wait()
-    local[2].wait()
     pl.semaphore_wait(barrier, 9)
     for distance in ALONG[0]:
         for way in (1, -1):
             send(64, PLACE[("A", -way * distance), 0], along(way * distance))
-    for side in (0, 1):
-        send(64 + side, PLACE[("B", 0), side], to_x)
+    send(64, PLACE[("B", 0), 0], to_x)
+    turned(1)
+    local[2].wait()
+    send(65, PLACE[("B", 0), 1], to_x)
     for way in (1, -1):
         send(65, PLACE[("A", -way), 1], along(way))
-
     local[3].wait()
     local[4].wait()
 

time: 41.5 us -> 41.5 us (level)
  no operation moved by 1% of the time
where the time goes in v7:
time: 41.5 us; the launch traced here: 41.3 us
  Pallas kernels  40 us (96%)
  local copies, waits for them, and re-layouts  1.37 us (3%)
    pallas_call x1, Pallas kernels, body(): pl.pallas_call(kernel, out_shape=jax.ShapeDtypeStruct(queries.shape, jnp....  40 us
    unnamed x5, local copies, waits for them, and re-layouts  1.37 us

profile of v7, /device:TPU:1, one launch (start us, length us, event | category | flops | bytes accessed | tf_op | source)
XLA Modules:
  0.0 41.3 jit_solution(2223603285004918311)
XLA Ops:
  0.0 0.0 copy-start
  0.0 0.0 copy-start.1
  0.0 0.7 %copy-done = s32[16]{0:T(128)S(1)} copy-done((s32[16]{0:T(128)S(1)}, s32[16]{0:T(128)}, u32[]{:S(2)}) %copy-start) | copy-done | bytes 88
  0.7 0.0 copy-done.1
  0.7 40.0 %shard_map.55 = bf16[4,256,128]{2,1,0:T(8,128)(2,1)S(1)} custom-call(bf16[4,256,128]{2,1,0:T(8,128)(2,1)} %q_ref.1, bf16[4,2,128,128]{3,2,1,0:T(8,128)(2,1)} %bitcast.2, bf16[4,2,128,128]{3,2,1,0:T(8,128)(2,1)} %bitcast.3, s32[16]{0:T(128)S(1)} %copy-done, s32[64]{0:T(128)S(1)} %copy-done.1), custom_call_target="tpu_custom_call" | custom-call | flops 4294967296 | bytes 1048576 | tf_op jit(solution)/shard_map/pallas_call | solution.py:279
  40.6 0.7 %copy.7 = bf16[4,256,128]{2,1,0:T(8,128)(2,1)} copy(bf16[4,256,128]{2,1,0:T(8,128)(2,1)S(1)} %shard_map.55) | data formatting | bytes 524288
Async XLA Ops:
  0.0 0.7 %copy-start = (s32[16]{0:T(128)S(1)}, s32[16]{0:T(128)}, u32[]{:S(2)}) copy-start(s32[16]{0:T(128)} %lens_in.1) | copy-start | bytes 196
  0.0 0.7 %copy-start.1 = (s32[64]{0:T(128)S(1)}, s32[64]{0:T(128)}, u32[]{:S(2)}) copy-start(s32[64]{0:T(128)} %order_in.1) | copy-start | bytes 772
